TPU v7x, 512 devices: a whole 4x8x8 slice. The times are simulated.
512 devices in a mesh: row: 32 (over z, x), col: 16 (over y, core).
Axes of the slice: x: 4, y: 8, z: 8, core: 2. Of those that a mesh axis runs over, the one named last changes fastest.
Arguments:
- trail_inverse: bfloat16 [12288, 12288], P('row', 'col'), may hold values from -6 to 6
- panels: bfloat16 [4, 12288, 512], P(None, 'row', 'col'), may hold values from -0.0625 to 0.0625
- couplings: bfloat16 [3, 512, 512], replicated, may hold values from -0.25 to 0.25
- diag_terms: float32 [4, 512, 512], P(None, None, 'col'), may hold values from -4 to 4
- listed: int32 [64], replicated, may hold values from 0 to 95, as said below
Outputs:
- panel_inverse: bfloat16 [4, 12288, 512], P(None, 'row', 'col')
- diag_inverse: float32 [4, 512, 512], P(None, None, 'col')
Inputs may be any that keep to these rules, and one draw needn't show every extreme that they name: `listed`: 64 distinct trailing block numbers, including 0 and 95.
All inputs are finite; a program needn't handle non-finite values.
Results may differ from a plain program's by a relative error of at most 0.0049.
Values may be sent and summed in bfloat16 or wider, within the bound.
A program may use at most 64 MiB of HBM per device.

v0:
```python
import jax
import jax.numpy as jnp
from jax import lax
from jax.sharding import PartitionSpec as P

BS = 128
SUPER = 4


def from_root(value, axis, source):
    kept = jnp.where(lax.axis_index(axis) == source, value, 0).astype(value.dtype)
    return lax.psum(kept, axis)


def listed_rows(listed, blk_row):
    first = lax.axis_index("row") * blk_row
    blocks = first + jnp.arange(blk_row, dtype=jnp.int32)
    listed_hit = jnp.any(listed[:, None] == blocks[None, :], axis=0)
    return jnp.repeat(listed_hit.astype(jnp.float32), BS)[:, None]


def on_device(trail_inverse, panels, couplings, diag_terms, listed):
    rows_local = trail_inverse.shape[0]
    narrow = panels.shape[2]
    row_mask = listed_rows(listed, rows_local // BS)
    col_index = lax.axis_index("col")
    ratio = lax.axis_size("row") // lax.axis_size("col")
    highest = lax.Precision.HIGHEST
    results = []
    diagonals = []
    prev_wide = None
    prev_block = None
    for step in range(SUPER):
        masked = (panels[step].astype(jnp.float32) * row_mask).astype(jnp.bfloat16)
        wide_panel = lax.all_gather(masked, "col", axis=1, tiled=True)
        pieces = [
            from_root(wide_panel, "row", ratio * col_index + offset) for offset in range(ratio)
        ]
        col_panel = jnp.concatenate(pieces, axis=0)
        product = jnp.dot(trail_inverse, col_panel, preferred_element_type=jnp.float32)
        summed = lax.psum_scatter(product, "col", scatter_dimension=1, tiled=True)
        if step > 0:
            carried = jnp.dot(prev_wide, couplings[step - 1], preferred_element_type=jnp.float32)
            summed = summed + lax.dynamic_slice_in_dim(carried, col_index * narrow, narrow, 1)
        result = (-(summed * row_mask)).astype(jnp.bfloat16)
        term = -lax.dot_general(
            wide_panel, result, (((0,), (0,)), ((), ())), preferred_element_type=jnp.float32
        )
        if step > 0:
            term = term + jnp.dot(carried.T, masked.astype(jnp.float32), precision=highest)
            coupling32 = couplings[step - 1].astype(jnp.float32)
        block_local = lax.psum(term, "row") + diag_terms[step]
        if step > 0:
            right_cols = lax.dynamic_slice_in_dim(coupling32, col_index * narrow, narrow, 1)
            inner = jnp.dot(prev_block, right_cols, precision=highest)
            block_local = block_local + jnp.dot(coupling32.T, inner, precision=highest)
        if step + 1 < SUPER:
            prev_block = lax.all_gather(block_local, "col", axis=1, tiled=True)
        if step + 1 < SUPER:
            prev_wide = lax.all_gather(result, "col", axis=1, tiled=True)
        results.append(result)
        diagonals.append(block_local)
    return (jnp.stack(results), jnp.stack(diagonals))


def solution(mesh):
    in_specs = (P("row", "col"), P(None, "row", "col"), P(), P(None, None, "col"), P())
    out_specs = (P(None, "row", "col"), P(None, None, "col"))
    return jax.shard_map(
        on_device, mesh=mesh, in_specs=in_specs, out_specs=out_specs, check_vma=False
    )
```

profile of v0, /device:TPU:1, one launch (start us, length us, event | category | flops | bytes accessed | tf_op | source)
XLA Modules:
  0.0 796.1 jit_solution(10402375917232824575)
XLA Ops:
  7.2 0.9 compare_reduce_fusion
  8.2 0.8 fusion.37
  9.1 22.0 %all_gather.30 = bf16[384,512]{0,1:T(8,128)(2,1)S(1)} all-gather(bf16[384,32]{0,1:T(8,128)(2,1)S(1)} %get-tuple-element.25), channel_id=1, replica_groups=mesh['row'=32,'col'=16] {'col'}, dimensions={1}, use_global_device_ids=true | all-gather | bytes 417792 | tf_op jit(solution)/shard_map/all_gather | solution.py:35
  31.1 17.1 %all_gather.31 = bf16[384,512]{0,1:T(8,128)(2,1)S(1)} all-gather(bf16[384,32]{0,1:T(8,128)(2,1)S(1)} %get-tuple-element.26), channel_id=1, replica_groups=mesh['row'=32,'col'=16] {'col'}, dimensions={1}, use_global_device_ids=true | all-gather | bytes 417792 | tf_op jit(solution)/shard_map/all_gather | solution.py:35
  48.2 15.5 %all_gather.33 = bf16[384,512]{0,1:T(8,128)(2,1)S(1)} all-gather(bf16[384,32]{0,1:T(8,128)(2,1)S(1)} %get-tuple-element.27), channel_id=1, replica_groups=mesh['row'=32,'col'=16] {'col'}, dimensions={1}, use_global_device_ids=true | all-gather | bytes 417792 | tf_op jit(solution)/shard_map/all_gather | solution.py:35
  63.7 16.9 %all_gather.35 = bf16[384,512]{0,1:T(8,128)(2,1)S(1)} all-gather(bf16[384,32]{0,1:T(8,128)(2,1)S(1)} %get-tuple-element.28), channel_id=1, replica_groups=mesh['row'=32,'col'=16] {'col'}, dimensions={1}, use_global_device_ids=true | all-gather | bytes 417792 | tf_op jit(solution)/shard_map/all_gather | solution.py:35
  80.6 1.0 broadcast_select_fusion.4
  81.6 1.0 broadcast_select_fusion.5
  82.5 1.0 broadcast_select_fusion.6
  83.5 1.0 broadcast_select_fusion.7
  84.5 166.3 %all-reduce.7.cloned.1.call-done = (bf16[384,512]{0,1:T(8,128)(2,1)}, bf16[384,512]{0,1:T(8,128)(2,1)}, bf16[384,512]{0,1:T(8,128)(2,1)}, bf16[384,512]{0,1:T(8,...) async-done(((bf16[384,512]{0,1:T(8,128)(2,1)}, bf16[384,512]{0,1:T(8,128)(2,1)}, ...) | async-done | bytes 3145744 | tf_op jit(solution)/shard_map/psum | solution.py:12
  250.8 2.7 convolution_bitcast_fusion.3
  253.6 1.5 convolution_bitcast_fusion.2
  255.2 1.5 convolution_bitcast_fusion.1
  256.8 1.5 convolution_bitcast_fusion
  258.3 54.0 %reduce-scatter.5.cloned.1.call-done = f32[384,32]{0,1:T(8,128)} async-done(((f32[384,512]{0,1:T(8,128)}), f32[384,32]{0,1:T(8,128)}) %reduce-scatter.5.cloned.1.call-update) | async-done | bytes 49168 | tf_op jit(solution)/shard_map/reduce_scatter | solution.py:41
  312.3 0.8 negate_convert_fusion.3
  313.7 17.5 %all_gather.32 = bf16[384,512]{0,1:T(8,128)(2,1)S(1)} all-gather(bf16[384,32]{0,1:T(8,128)(2,1)S(1)} %negate_convert_fusion.3), channel_id=1, replica_groups=mesh['row'=32,'col'=16] {'col'}, dimensions={1}, use_global_device_ids=true | all-gather | bytes 417792 | tf_op jit(solution)/shard_map/all_gather | solution.py:60
  331.8 0.7 copy.13
  332.5 41.1 %reduce-scatter.7.cloned.1.call-done = f32[384,32]{0,1:T(8,128)} async-done(((f32[384,512]{0,1:T(8,128)}), f32[384,32]{0,1:T(8,128)}) %reduce-scatter.7.cloned.1.call-update) | async-done | bytes 49168 | tf_op jit(solution)/shard_map/reduce_scatter | solution.py:41
  373.5 0.8 negate_convert_fusion.2
  375.0 17.5 %all_gather.34 = bf16[384,512]{0,1:T(8,128)(2,1)S(1)} all-gather(bf16[384,32]{0,1:T(8,128)(2,1)S(1)} %negate_convert_fusion.2), channel_id=1, replica_groups=mesh['row'=32,'col'=16] {'col'}, dimensions={1}, use_global_device_ids=true | all-gather | bytes 417792 | tf_op jit(solution)/shard_map/all_gather | solution.py:60
  392.9 0.9 copy-done.2
  393.9 0.7 copy.14
  394.6 40.2 %reduce-scatter.9.cloned.1.call-done = f32[384,32]{0,1:T(8,128)} async-done(((f32[384,512]{0,1:T(8,128)}), f32[384,32]{0,1:T(8,128)}) %reduce-scatter.9.cloned.1.call-update) | async-done | bytes 49168 | tf_op jit(solution)/shard_map/reduce_scatter | solution.py:41
  434.8 0.8 negate_convert_fusion.1
  436.3 17.5 %all_gather.36 = bf16[384,512]{0,1:T(8,128)(2,1)S(1)} all-gather(bf16[384,32]{0,1:T(8,128)(2,1)S(1)} %negate_convert_fusion.1), channel_id=1, replica_groups=mesh['row'=32,'col'=16] {'col'}, dimensions={1}, use_global_device_ids=true | all-gather | bytes 417792 | tf_op jit(solution)/shard_map/all_gather | solution.py:60
  454.2 0.9 copy-done.4
  455.9 1.9 convolution_negate_fusion.3
  457.8 1.2 convolution_negate_fusion.2
  459.1 1.2 convolution_negate_fusion.1
  460.3 1.8 convolution_add_fusion.2
  462.1 1.0 convolution_add_fusion.1
  463.1 32.9 %reduce-scatter.11.cloned.1.call-done = f32[384,32]{0,1:T(8,128)} async-done(((f32[384,512]{0,1:T(8,128)}), f32[384,32]{0,1:T(8,128)}) %reduce-scatter.11.cloned.1.call-update) | async-done | bytes 49168 | tf_op jit(solution)/shard_map/reduce_scatter | solution.py:41
  496.0 0.8 negate_convert_fusion
  497.0 2.1 convolution_add_fusion
  499.3 153.7 %all-reduce.5.cloned.1.call-done = (f32[512,32]{0,1:T(8,128)}, f32[512,32]{0,1:T(8,128)}, f32[512,32]{0,1:T(8,128)}, f32[512,32]{0,1:T(8,128)}) async-done(((f32[512,32]{0,1:T(8,128)}, f32[512,32]{0,1:T(8,128)}, f32[512,32]{0,1:T(8,128)}, f32[512,32]{0,1:T(8,128)}), (f32[512,32]{0,1:T(8,128)}, f32[512,32]{0,1:T(8,128)}, f32[512,32]{0,1:T(8,128)}, f32[512,32]{0,1:T(8,128)})) %all-reduce.5.cloned.1.call-update) | async-done | bytes 262160 | tf_op jit(solution)/shard_map/psum | solution.py:52
  653.0 1.5 bitcast_add_fusion.3
  654.6 1.1 fusion.51
  655.7 42.8 %all-gather.4.cloned.1.call-done = f32[512,512]{0,1:T(8,128)} async-done(((f32[512,32]{0,1:T(8,128)}), f32[512,512]{0,1:T(8,128)}) %all-gather.4.cloned.1.call-update) | async-done | bytes 1048592 | tf_op jit(solution)/shard_map/all_gather | solution.py:58
  698.4 2.3 fusion.29
  700.8 1.0 fusion.3
  701.9 40.0 %all-gather.6.cloned.1.call-done = f32[512,512]{0,1:T(8,128)} async-done(((f32[512,32]{0,1:T(8,128)}), f32[512,512]{0,1:T(8,128)}) %all-gather.6.cloned.1.call-update) | async-done | bytes 1048592 | tf_op jit(solution)/shard_map/all_gather | solution.py:58
  741.9 2.3 fusion.27
  744.2 1.0 fusion.2
  745.9 39.3 %all-gather.8.cloned.1.call-done = f32[512,512]{0,1:T(8,128)} async-done(((f32[512,32]{0,1:T(8,128)}), f32[512,512]{0,1:T(8,128)}) %all-gather.8.cloned.1.call-update) | async-done | bytes 1048592 | tf_op jit(solution)/shard_map/all_gather | solution.py:58
  785.3 2.3 fusion.25
  787.5 1.2 fusion.1
  (98 shorter events, 6.4 us)
Async XLA Ops:
  7.2 243.6 %copy-start = (bf16[384,768]{1,0:T(8,128)(2,1)S(1)}, bf16[384,768]{1,0:T(8,128)(2,1)}, u32[]{:S(2)}) copy-start(bf16[384,768]{1,0:T(8,128)(2,1)} %param.5) | copy-start | bytes 1769476
  7.2 243.6 %all-reduce.7.cloned.1.call-start = ((), (), s32[]{:S(2)}) async-start(), calls=%async_computation.12 | async-start | bytes 6291456 | tf_op jit(solution)/shard_map/psum | solution.py:12
  8.2 426.6 %copy-start.24 = (f32[384]{0:T(512)}, f32[384]{0:T(512)S(1)}, u32[]{:S(2)}) copy-start(f32[384]{0:T(512)S(1)} %broadcast_bitcast_fusion) | copy-start | bytes 4612
  9.0 54.7 %copy-start.18 = (bf16[384,32]{0,1:T(8,128)(2,1)}, bf16[384,32]{0,1:T(8,128)(2,1)S(1)}, u32[]{:S(2)}) copy-start(bf16[384,32]{0,1:T(8,128)(2,1)S(1)} %get-tuple-element.27) | copy-start | bytes 73732
  9.0 54.7 %copy-start.20 = (bf16[384,32]{0,1:T(8,128)(2,1)}, bf16[384,32]{0,1:T(8,128)(2,1)S(1)}, u32[]{:S(2)}) copy-start(bf16[384,32]{0,1:T(8,128)(2,1)S(1)} %get-tuple-element.26) | copy-start | bytes 73732
  9.1 54.7 %copy-start.16 = (bf16[384,32]{0,1:T(8,128)(2,1)}, bf16[384,32]{0,1:T(8,128)(2,1)S(1)}, u32[]{:S(2)}) copy-start(bf16[384,32]{0,1:T(8,128)(2,1)S(1)} %get-tuple-element.28) | copy-start | bytes 73732
  31.1 52.4 %copy-start.7 = (bf16[384,512]{0,1:T(8,128)(2,1)}, bf16[384,512]{0,1:T(8,128)(2,1)S(1)}, u32[]{:S(2)}) copy-start(bf16[384,512]{0,1:T(8,128)(2,1)S(1)} %all_gather.30) | copy-start | bytes 1179652
  48.2 34.4 %copy-start.6 = (bf16[384,512]{0,1:T(8,128)(2,1)}, bf16[384,512]{0,1:T(8,128)(2,1)S(1)}, u32[]{:S(2)}) copy-start(bf16[384,512]{0,1:T(8,128)(2,1)S(1)} %all_gather.31) | copy-start | bytes 1179652
  63.7 19.8 %copy-start.5 = (bf16[384,512]{0,1:T(8,128)(2,1)}, bf16[384,512]{0,1:T(8,128)(2,1)S(1)}, u32[]{:S(2)}) copy-start(bf16[384,512]{0,1:T(8,128)(2,1)S(1)} %all_gather.33) | copy-start | bytes 1179652
  84.5 227.8 %reduce-scatter.5.cloned.1.call-start = ((), (), s32[]{:S(2)}) async-start(), calls=%async_computation.4 | async-start | bytes 835584 | tf_op jit(solution)/shard_map/reduce_scatter | solution.py:41
  250.8 2.8 copy-start.32
  250.8 2.8 copy-start.33
  253.5 120.0 %reduce-scatter.7.cloned.1.call-start = ((), (), s32[]{:S(2)}) async-start(), calls=%async_computation.5 | async-start | bytes 835584 | tf_op jit(solution)/shard_map/reduce_scatter | solution.py:41
  253.6 1.6 copy-start.30
  253.6 1.6 copy-start.31
  255.1 179.7 %reduce-scatter.9.cloned.1.call-start = ((), (), s32[]{:S(2)}) async-start(), calls=%async_computation.6 | async-start | bytes 835584 | tf_op jit(solution)/shard_map/reduce_scatter | solution.py:41
  255.1 1.6 copy-start.28
  255.2 1.6 copy-start.29
  256.7 239.3 %reduce-scatter.11.cloned.1.call-start = ((), (), s32[]{:S(2)}) async-start(), calls=%async_computation.7 | async-start | bytes 835584 | tf_op jit(solution)/shard_map/reduce_scatter | solution.py:41
  256.8 74.5 %copy-start.1 = (bf16[3,512,512]{2,1,0:T(8,128)(2,1)S(1)}, bf16[3,512,512]{2,1,0:T(8,128)(2,1)}, u32[]{:S(2)}) copy-start(bf16[3,512,512]{2,1,0:T(8,128)(2,1)} %param.7) | copy-start | bytes 4718596
  258.3 394.7 %all-reduce.5.cloned.1.call-start = ((), (), s32[]{:S(2)}) async-start(), calls=%async_computation.11 | async-start | bytes 524288 | tf_op jit(solution)/shard_map/psum | solution.py:52
  313.1 0.6 copy-start.21
  374.4 0.6 copy-start.11
  392.9 0.9 copy-start.2
  435.6 0.6 copy-start.13
  454.2 0.9 copy-start.4
  455.9 6.2 copy-start.3
  455.9 6.2 copy-start.19
  455.9 40.1 %copy-start.23 = (f32[384,32]{0,1:T(8,128)S(1)}, f32[384,32]{0,1:T(8,128)}, u32[]{:S(2)}) copy-start(f32[384,32]{0,1:T(8,128)} %copy.15) | copy-start | bytes 147460
  459.1 38.0 %copy-start.17 = (bf16[384,32]{0,1:T(8,128)(2,1)S(1)}, bf16[384,32]{0,1:T(8,128)(2,1)}, u32[]{:S(2)}) copy-start(bf16[384,32]{0,1:T(8,128)(2,1)} %copy-done.16) | copy-start | bytes 73732
  462.1 190.9 %copy-start.15 = (f32[4,512,32]{1,2,0:T(8,128)S(1)}, f32[4,512,32]{1,2,0:T(8,128)}, u32[]{:S(2)}) copy-start(f32[4,512,32]{1,2,0:T(8,128)} %param.8) | copy-start | bytes 786436
  499.2 199.2 %all-gather.4.cloned.1.call-start = ((), (), s32[]{:S(2)}) async-start(), calls=%async_computation.8 | async-start | bytes 1114112 | tf_op jit(solution)/shard_map/all_gather | solution.py:58
  654.5 46.2 %copy-start.27 = (f32[512,32]{0,1:T(8,128)S(1)}, f32[512,32]{0,1:T(8,128)}, u32[]{:S(2)}) copy-start(f32[512,32]{0,1:T(8,128)} %get-tuple-element.3) | copy-start | bytes 196612
  654.5 87.4 %all-gather.6.cloned.1.call-start = ((), (), s32[]{:S(2)}) async-start(), calls=%async_computation.9 | async-start | bytes 1114112 | tf_op jit(solution)/shard_map/all_gather | solution.py:58
  700.7 43.4 %copy-start.26 = (f32[512,32]{0,1:T(8,128)S(1)}, f32[512,32]{0,1:T(8,128)}, u32[]{:S(2)}) copy-start(f32[512,32]{0,1:T(8,128)} %get-tuple-element.4) | copy-start | bytes 196612
  700.8 44.5 %copy-start.22 = (f32[384,32]{0,1:T(8,128)S(1)}, f32[384,32]{0,1:T(8,128)}, u32[]{:S(2)}) copy-start(f32[384,32]{0,1:T(8,128)} %reduce-scatter.5.cloned.1.call-done) | copy-start | bytes 147460
  700.8 44.5 %copy-start.25 = (f32[384]{0:T(512)S(1)}, f32[384]{0:T(512)}, u32[]{:S(2)}) copy-start(f32[384]{0:T(512)} %copy-done.24) | copy-start | bytes 4612
  700.8 44.5 %copy-start.12 = (bf16[384,32]{0,1:T(8,128)(2,1)S(1)}, bf16[384,32]{0,1:T(8,128)(2,1)}, u32[]{:S(2)}) copy-start(bf16[384,32]{0,1:T(8,128)(2,1)} %copy-done.11) | copy-start | bytes 73732
  700.8 44.5 %copy-start.14 = (bf16[384,32]{0,1:T(8,128)(2,1)S(1)}, bf16[384,32]{0,1:T(8,128)(2,1)}, u32[]{:S(2)}) copy-start(bf16[384,32]{0,1:T(8,128)(2,1)} %copy-done.13) | copy-start | bytes 73732
  701.8 83.4 %all-gather.8.cloned.1.call-start = ((), (), s32[]{:S(2)}) async-start(), calls=%async_computation.10 | async-start | bytes 1114112 | tf_op jit(solution)/shard_map/all_gather | solution.py:58
  745.2 43.6 %copy-start.8 = (f32[512,32]{0,1:T(8,128)S(1)}, f32[512,32]{0,1:T(8,128)}, u32[]{:S(2)}) copy-start(f32[512,32]{0,1:T(8,128)} %bitcast_add_fusion.3) | copy-start | bytes 196612
  745.2 43.6 %copy-start.9 = (f32[512,32]{0,1:T(8,128)S(1)}, f32[512,32]{0,1:T(8,128)}, u32[]{:S(2)}) copy-start(f32[512,32]{0,1:T(8,128)} %fusion.3) | copy-start | bytes 196612
  745.2 43.6 %copy-start.10 = (f32[512,32]{0,1:T(8,128)S(1)}, f32[512,32]{0,1:T(8,128)}, u32[]{:S(2)}) copy-start(f32[512,32]{0,1:T(8,128)} %fusion.2) | copy-start | bytes 196612
Sparse Core Ops, SparseCore 0:
  84.6 166.1 all-reduce.6
  253.8 58.4 reduce-scatter.4
  315.1 58.3 reduce-scatter.6
  376.4 58.3 reduce-scatter.8
  437.4 58.4 reduce-scatter.10
  500.8 152.1 all-reduce.4
  655.9 42.4 all-gather.3
  702.0 39.8 all-gather.5
  745.3 39.8 all-gather.7
where the time goes:
time: 797 us; the launch traced here: 796 us
  waiting for transfers between devices  610 us (77%)
  blocking collectives  124 us (16%)
  matrix products  27.9 us (4%)
  between operations  14.3 us (2%)
  other arithmetic  11.7 us (1%)
    reduce_scatter x4, waiting for transfers between devices, on_device(): summed = lax.psum_scatter(product, 'col', scatter_dimension=1, tiled=True)  168 us
    psum x1, waiting for transfers between devices, from_root(): return lax.psum(kept, axis)  166 us
    psum x1, waiting for transfers between devices, on_device(): block_local = lax.psum(term, 'row') + diag_terms[step]  154 us
    all_gather x3, waiting for transfers between devices, on_device(): prev_block = lax.all_gather(block_local, 'col', axis=1, tiled=True)  122 us
    all_gather x4, blocking collectives, on_device(): wide_panel = lax.all_gather(masked, 'col', axis=1, tiled=True)  71.5 us
    all_gather x3, blocking collectives, on_device(): prev_wide = lax.all_gather(result, 'col', axis=1, tiled=True)  52.5 us
  transfers between devices with their start and end apart: 9, of which 9 were waited for; matrix products, arithmetic and copies ran while one was open for 2% of the time, Pallas kernels for 0%

commit v1 on v0

v1 whole, which is shorter than its diff:
```python
import functools

import jax
import jax.numpy as jnp
from jax import lax
from jax.experimental import pallas as pl
from jax.experimental.pallas import tpu as pltpu
from jax.sharding import PartitionSpec as P

SUPER = 4
NX = 4
ROWS = 384
PIECE = 128
LAG = 2
MESH = pl.DeviceIdType.MESH
F32 = jnp.float32
BF16 = jnp.bfloat16
NT_DIMS = (((1,), (1,)), ((), ()))
TN_DIMS = (((0,), (0,)), ((), ()))


def iota(shape, dim):
    return lax.broadcasted_iota(jnp.int32, shape, dim)


def mod(value, size):
    return lax.rem(value + 2 * size, size)


def swap_halves(value):
    return pltpu.roll(value, 64, 1)


def kernel(
    ny,
    panels_ref, listed_ref, trail_ref, coup_ref, diag_ref,
    outp_ref, outd_ref,
    tp, cc, ct, vst, dgo, dgs, dgw, mw, ms, sp, rb, ss, zs, zb, zo, ps, pb, ev, eb1, eb2, fb,
    sem, zrecv, xrecv,
):
    nz = ny
    width = 64 * ny
    chain_rows = ROWS // ny
    tiles = width // 128
    row, col = lax.axis_index("row"), lax.axis_index("col")
    z, x = lax.div(row, NX), lax.rem(row, NX)
    y, h = lax.div(col, 2), lax.rem(col, 2)
    sibling = 1 - h

    def dev(xx, yy, zz, hh):
        return (zz * NX + xx, yy * 2 + hh)

    def remote(src, dst, send, recv, device):
        return pltpu.make_async_remote_copy(
            src_ref=src, dst_ref=dst, send_sem=send, recv_sem=recv,
            device_id=device, device_id_type=MESH,
        )

    def wait_bytes(ref, semaphore):
        pltpu.make_async_copy(ref, ref, semaphore).wait()

    (s_t, r_t, s_z, s_x, s_mw, r_mw, s_tp, r_tp, s_rs, r_rs, s_ss, r_ss, s_zb, r_zb,
     s_mf, r_mf, s_zo, r_zo, s_p, r_p, s_e, r_e1, r_e2, s_f, r_f, s_dg, r_dg,
     l_tp, l_cc, l_dg) = [sem.at[i] for i in range(30)]

    barrier = pltpu.get_barrier_semaphore()

    def greet(device):
        pl.semaphore_signal(barrier, inc=1, device_id=device, device_id_type=MESH)

    @pl.loop(1, 2 * ny)
    def _(step):
        greet((row, mod(col + step, 2 * ny)))

    @pl.loop(1, NX * nz)
    def _(step):
        greet((mod(row + step, NX * nz), col))

    @pl.when(y != z)
    def _():
        greet(dev(x, z, y, h))

    @pl.loop(0, nz)
    def _(zz):
        me = jnp.logical_and(jnp.logical_and(z == y, zz == z), h == 1)

        @pl.when(jnp.logical_not(me))
        def _():
            greet(dev(x, z, zz, 1))

    own_tp = pltpu.make_async_copy(trail_ref, tp.at[h], l_tp)
    own_tp.start()
    own_cc = pltpu.make_async_copy(coup_ref, cc, l_cc)
    own_cc.start()
    own_dg = pltpu.make_async_copy(diag_ref.at[x, pl.ds(64 * z, 64)], dgo, l_dg)
    own_dg.start()

    listed = listed_ref[...]

    def flag(block):
        return jnp.max(jnp.where(listed == block, 1.0, 0.0), axis=1, keepdims=True)

    lane = iota((1, ROWS), 1)
    piece_mask = jnp.where(
        lane < 128, flag(3 * row), jnp.where(lane < 256, flag(3 * row + 1), flag(3 * row + 2))
    )
    eye = jnp.where(iota((32, 32), 0) == iota((32, 32), 1), 1.0, 0.0).astype(BF16)
    for k in range(SUPER):
        turned = lax.dot_general(eye, panels_ref[k], NT_DIMS, preferred_element_type=F32)
        mw[h, y, 32 * k:32 * (k + 1), :] = (turned * piece_mask).astype(BF16)

    off_diagonal = jnp.where(y != z, 1, 0)
    pl.semaphore_wait(
        barrier,
        (2 * ny - 1) + (NX * nz - 1) + off_diagonal + h * (2 * ny - 1 + off_diagonal),
    )

    mine = mw.at[h, y]

    @pl.when(y != z)
    def _():
        remote(mine, ms.at[y * NX + x], s_t, r_t, dev(x, z, y, h)).start()

    @pl.when(y == z)
    def _():
        pltpu.make_async_copy(mine, ms.at[y * NX + x], r_t).start()

    send_tp = remote(trail_ref, tp.at[h], s_tp, r_tp, dev(x, y, z, sibling))
    send_tp.start()
    send_dg = remote(
        diag_ref.at[x, pl.ds(64 * z, 64)], dgs, s_dg, r_dg, dev(x, y, z, sibling)
    )
    send_dg.start()

    def near(step):
        half = lax.div(step + 1, 2)
        return jnp.where(lax.rem(step, 2) == 1, half, mod(-half, nz))

    home = ms.at[z * NX + x]
    wait_bytes(home, r_t)

    @pl.loop(1, nz)
    def _(step):
        delta = near(step)
        remote(home, home, s_z, zrecv.at[delta], dev(x, y, mod(z + delta, nz), h)).start()

    @pl.loop(1, ny)
    def _(step):
        remote(mine, mine, s_mw, r_mw, dev(x, mod(y + near(step), ny), z, h)).start()

    own_tp.wait()
    wait_bytes(tp.at[0], r_tp)

    @pl.loop(0, nz + LAG)
    def _(step):
        @pl.when(step < nz)
        def _():
            delta = near(step)
            slot = ms.at[mod(z - delta, nz) * NX + x]

            @pl.when(step > 0)
            def _():
                wait_bytes(slot, zrecv.at[delta])

            for dx in (1, 3, 2):
                remote(
                    slot, slot, s_x, xrecv.at[delta], dev(mod(x + dx, NX), y, z, h)
                ).start()

        @pl.when(step >= LAG)
        def _():
            delta = near(step - LAG)
            chunk = mod(z - delta, nz)
            wait_bytes(ms.at[pl.ds(0, NX - 1)], xrecv.at[delta])
            total = None
            for xx in range(NX):
                term = lax.dot_general(
                    tp[xx // 2, :, ROWS * (xx % 2):ROWS * (xx % 2 + 1)],
                    ms[chunk * NX + xx], NT_DIMS, preferred_element_type=F32,
                )
                total = term if total is None else total + term
            total = total.astype(BF16)
            lanes = pl.ds(pl.multiple_of(chunk * PIECE, PIECE), PIECE)
            for yy in range(ny):
                sp[yy, :, lanes] = total[chain_rows * yy:chain_rows * (yy + 1)]

            @pl.loop(1, ny)
            def _(i):
                to = mod(y + i, ny)
                remote(
                    sp.at[to, :, lanes], rb.at[i - 1, :, lanes], s_rs, r_rs, dev(x, to, z, h)
                ).start()

    own_cc.wait()
    wide_eye = jnp.where(iota((width, width), 0) == iota((width, width), 1), 1.0, 0.0)
    wide_eye = wide_eye.astype(BF16)
    group = lax.div(iota((width, 128), 1), 32)
    picks = iota((width, 128), 0) == col * 32 + lax.rem(iota((width, 128), 1), 32)
    for j in range(SUPER - 1):
        ct[j] = lax.dot_general(
            wide_eye, cc[j], NT_DIMS, preferred_element_type=F32
        ).astype(BF16)
    above = None
    for j in reversed(range(SUPER)):
        chosen = jnp.where(jnp.logical_and(picks, group == j), 1.0, 0.0)
        if above is not None:
            chosen = chosen + jnp.dot(cc[j], above, preferred_element_type=F32)
        above = chosen.astype(BF16)
        vst[j] = above

    own_dg.wait()
    wait_bytes(dgs, r_dg)
    dgw[...] = jnp.zeros_like(dgw)
    dgw[0, :, 0:32] = dgo[...]
    dgw[1, :, 0:32] = dgs[...]
    both = dgw[0] + pltpu.roll(dgw[1], 32, 1)
    diag_packed = both[0:32] + swap_halves(both[32:64])

    wait_bytes(mw.at[0, pl.ds(0, ny - 1)], r_mw)
    send_mf = remote(mw.at[h], mw.at[h], s_mf, r_mf, dev(x, y, z, sibling))
    send_mf.start()

    wait_bytes(rb, r_rs)
    for t in range(ny):
        part = slice(128 * t, 128 * (t + 1))
        total = sp[y, :, part].astype(F32)
        for i in range(ny - 1):
            total = total + rb[i, :, part].astype(F32)
        ss[h, :, part] = total
    send_ss = remote(ss.at[h], ss.at[h], s_ss, r_ss, dev(x, y, z, sibling))
    send_ss.start()
    wait_bytes(ss.at[0], r_ss)

    block = lax.shift_right_logical(
        ROWS * row + chain_rows * y + iota((chain_rows, 1), 0), 7
    )
    row_mask = jnp.max(jnp.where(listed == block, 1.0, 0.0), axis=1, keepdims=True)
    quarter = lax.div(iota((chain_rows, 128), 1), 32)
    low = iota((chain_rows, 128), 1) < 64
    result = None
    kept = []
    for k in range(SUPER):
        found = []
        for t in range(tiles):
            tile = None
            for g in range(4):
                yy = 2 * t + g // 2
                source = ss[g % 2, :, 128 * yy:128 * (yy + 1)]
                shift = (32 * (g - k)) % 128
                if shift:
                    source = pltpu.roll(source, shift, 1)
                tile = source if tile is None else jnp.where(quarter == g, source, tile)
            found.append(tile)
        summed = jnp.concatenate(found, axis=1) if tiles > 1 else found[0]
        carried = jnp.zeros_like(summed)
        if k > 0:
            carried = jnp.dot(result, cc[k - 1], preferred_element_type=F32)
            summed = summed + carried
        result = (-(summed * row_mask)).astype(BF16)
        kept.append(jnp.where(h == 0, result.astype(F32), carried))
    for pair in range(SUPER // 2):
        for t in range(tiles):
            part = slice(128 * t, 128 * (t + 1))
            first, second = kept[2 * pair][:, part], kept[2 * pair + 1][:, part]
            lanes = slice(128 * pair, 128 * (pair + 1))
            zs[2 * t, :, lanes] = jnp.where(low, first, swap_halves(second)).astype(BF16)
            zs[2 * t + 1, :, lanes] = jnp.where(low, swap_halves(first), second).astype(BF16)

    own_rows = pl.ds(pl.multiple_of(chain_rows * y, 16), chain_rows)

    @pl.loop(1, ny)
    def _(i):
        to = mod(y + i, ny)
        remote(zs.at[to], zb.at[own_rows], s_zb, r_zb, dev(x, to, z, h)).start()

    zb[own_rows, :] = zs[y]
    wait_bytes(mw.at[0], r_mf)
    wait_bytes(zb.at[pl.ds(0, chain_rows * (ny - 1))], r_zb)

    @pl.when(h == 0)
    def _():
        remote(zb, zo, s_zo, r_zo, dev(x, y, z, 1)).start()

    low32 = iota((32, 128), 1) < 64
    for k in range(SUPER):
        left = jnp.concatenate(
            [mw[c % 2, c // 2, 32 * k:32 * (k + 1), :] for c in range(2 * ny)], axis=0
        )
        pair = k // 2
        product = jnp.dot(
            left, zb[:, 128 * pair:128 * (pair + 1)], preferred_element_type=F32
        )
        for zz in range(nz):
            upper = product[64 * zz:64 * zz + 32]
            lower = product[64 * zz + 32:64 * zz + 64]
            if k % 2 == 0:
                packed = jnp.where(low32, upper, swap_halves(lower))
            else:
                packed = jnp.where(low32, swap_halves(upper), lower)
            ps[k * nz + zz] = packed.astype(BF16)

    @pl.loop(1, NX * nz)
    def _(i):
        xx = mod(x + lax.div(i, nz), NX)
        zz = mod(z + lax.rem(i, nz), nz)
        remote(ps.at[xx * nz + zz], pb.at[i - 1], s_p, r_p, dev(xx, y, zz, h)).start()

    @pl.when(h == 0)
    def _():
        for k in range(SUPER):
            tile = zb[:, 128 * (k // 2):128 * (k // 2 + 1)].astype(F32)
            tile = swap_halves(tile) if k % 2 else tile
            outp_ref[k] = tile[:, 0:32].astype(BF16)

    @pl.when(h == 1)
    def _():
        wait_bytes(zo, r_zo)
        for k in range(SUPER):
            tile = zo[:, 128 * (k // 2):128 * (k // 2 + 1)].astype(F32)
            tile = pltpu.roll(tile, 32 if k % 2 else 96, 1)
            outp_ref[k] = tile[:, 0:32].astype(BF16)

    wait_bytes(pb, r_p)
    total = ps[x * nz + z].astype(F32)
    for i in range(NX * nz - 1):
        total = total + pb[i].astype(F32)
    ev[...] = jnp.where(h == 0, diag_packed - total, total).astype(BF16)

    @pl.loop(0, 2 * ny)
    def _(i):
        yy, hh = lax.div(i, 2), lax.rem(i, 2)

        @pl.when(h == 0)
        def _():
            @pl.when(i == col)
            def _():
                pltpu.make_async_copy(ev, eb1.at[y], r_e1).start()

            @pl.when(i != col)
            def _():
                remote(ev, eb1.at[y], s_e, r_e1, dev(x, yy, z, hh)).start()

        @pl.when(h == 1)
        def _():
            me = jnp.logical_and(i == col, y == z)

            @pl.when(me)
            def _():
                pltpu.make_async_copy(ev, eb2.at[z], r_e2).start()

            @pl.when(jnp.logical_not(me))
            def _():
                remote(ev, eb2.at[z], s_e, r_e2, dev(x, yy, y, hh)).start()

    wait_bytes(eb1, r_e1)
    wait_bytes(eb2, r_e2)
    upper, lower = [], []
    for t in range(tiles):
        first, second = eb1[2 * t].astype(F32), eb1[2 * t + 1].astype(F32)
        upper.append(jnp.where(low32, first, swap_halves(second)))
        lower.append(jnp.where(low32, swap_halves(first), second))
    if tiles > 1:
        upper = jnp.concatenate(upper, axis=1)
        lower = jnp.concatenate(lower, axis=1)
    else:
        upper, lower = upper[0], lower[0]
    straight = jnp.concatenate([upper, lower], axis=0).astype(BF16)
    stack = []
    for b in range(nz):
        value = eb2[b].astype(F32)
        stack += [value, swap_halves(value)]
    stack = jnp.concatenate(stack, axis=0).astype(BF16)
    right = vst[x]
    turned = lax.dot_general(stack, right, TN_DIMS, preferred_element_type=F32)
    own = jnp.dot(straight, right, preferred_element_type=F32) + turned[0:64]
    mine_f = fb.at[x * nz + z]
    mine_f[...] = own.astype(BF16)

    @pl.loop(1, NX * nz)
    def _(i):
        xx = mod(x + lax.div(i, nz), NX)
        zz = mod(z + lax.rem(i, nz), nz)
        remote(mine_f, mine_f, s_f, r_f, dev(xx, y, zz, h)).start()

    wait_bytes(fb.at[pl.ds(0, NX * nz - 1)], r_f)
    state = fb[pl.ds(0, nz)].reshape(width, 128).astype(F32)
    for j in range(SUPER - 1):
        high = state.astype(BF16)
        rest = (state - high.astype(F32)).astype(BF16)
        moved = jnp.dot(
            ct[j], jnp.concatenate([high, rest], axis=1), preferred_element_type=F32
        )
        moved = moved[:, 0:128] + moved[:, 128:256]
        added = fb[pl.ds((j + 1) * nz, nz)].reshape(width, 128).astype(F32)
        state = added + jnp.where(group > j, moved, state)
    for k in range(SUPER):
        outd_ref[k] = (pltpu.roll(state, 128 - 32 * k, 1) if k else state)[:, 0:32]

    @pl.when(y != z)
    def _():
        wait_bytes(home, s_t)

    wait_bytes(tp.at[0], s_tp)
    wait_bytes(dgs, s_dg)
    wait_bytes(ms.at[pl.ds(0, nz - 1)], s_z)
    wait_bytes(mw.at[0, pl.ds(0, ny - 1)], s_mw)
    wait_bytes(ms.at[pl.ds(0, (NX - 1) * nz)], s_x)
    wait_bytes(rb, s_rs)
    wait_bytes(mw.at[0], s_mf)
    wait_bytes(ss.at[0], s_ss)
    wait_bytes(zb.at[pl.ds(0, chain_rows * (ny - 1))], s_zb)

    @pl.when(h == 0)
    def _():
        wait_bytes(zo, s_zo)

    wait_bytes(pb, s_p)
    wait_bytes(eb1.at[pl.ds(0, ny - 1)], s_e)
    wait_bytes(eb2.at[pl.ds(0, ny - 1)], s_e)

    wait_bytes(ev, s_e)

    @pl.when(jnp.logical_and(h == 1, y != z))
    def _():
        wait_bytes(ev, s_e)

    wait_bytes(fb.at[pl.ds(0, NX * nz - 1)], s_f)


def on_device(trail_inverse, panels, couplings, diag_terms, listed):
    ny = lax.axis_size("col") // 2
    nz = ny
    width = 64 * ny
    chain_rows = ROWS // ny
    vmem = pl.BlockSpec(memory_space=pltpu.VMEM)
    anywhere = pl.BlockSpec(memory_space=pl.ANY)
    return pl.pallas_call(
        functools.partial(kernel, ny),
        out_shape=(
            jax.ShapeDtypeStruct((SUPER, ROWS, 32), BF16),
            jax.ShapeDtypeStruct((SUPER, width, 32), F32),
        ),
        in_specs=[vmem, vmem, anywhere, anywhere, anywhere],
        out_specs=(vmem, vmem),
        scratch_shapes=[
            pltpu.VMEM((2, ROWS, 768), BF16),
            pltpu.VMEM((SUPER - 1, width, width), BF16),
            pltpu.VMEM((SUPER - 1, width, width), BF16),
            pltpu.VMEM((SUPER, width, 128), BF16),
            pltpu.VMEM((64, 32), F32),
            pltpu.VMEM((64, 32), F32),
            pltpu.VMEM((2, 64, 128), F32),
            pltpu.VMEM((2, ny, PIECE, ROWS), BF16),
            pltpu.VMEM((nz * NX, PIECE, ROWS), BF16),
            pltpu.VMEM((ny, chain_rows, 128 * ny), BF16),
            pltpu.VMEM((ny - 1, chain_rows, 128 * ny), BF16),
            pltpu.VMEM((2, chain_rows, 128 * ny), F32),
            pltpu.VMEM((ny, chain_rows, 256), BF16),
            pltpu.VMEM((ROWS, 256), BF16),
            pltpu.VMEM((ROWS, 256), BF16),
            pltpu.VMEM((NX * nz, 32, 128), BF16),
            pltpu.VMEM((NX * nz - 1, 32, 128), BF16),
            pltpu.VMEM((32, 128), BF16),
            pltpu.VMEM((ny, 32, 128), BF16),
            pltpu.VMEM((nz, 32, 128), BF16),
            pltpu.VMEM((NX * nz, 64, 128), BF16),
            pltpu.SemaphoreType.DMA((30,)),
            pltpu.SemaphoreType.DMA((nz,)),
            pltpu.SemaphoreType.DMA((nz,)),
        ],
        compiler_params=pltpu.CompilerParams(
            collective_id=0, has_side_effects=True, vmem_limit_bytes=48 * 1024 * 1024
        ),
        name="chain",
    )(panels, listed.reshape(1, -1), trail_inverse, couplings, diag_terms)


def solution(mesh):
    in_specs = (P("row", "col"), P(None, "row", "col"), P(), P(None, None, "col"), P())
    out_specs = (P(None, "row", "col"), P(None, None, "col"))
    return jax.shard_map(
        on_device, mesh=mesh, in_specs=in_specs, out_specs=out_specs, check_vma=False
    )
```

time: 797 us -> 124 us (0.16)
  waiting for transfers between devices: 610 us -> 0 us
  blocking collectives: 124 us -> 0 us
  Pallas kernels: 0 us -> 115 us
  matrix products: 27.9 us -> 0 us
  between operations: 14.3 us -> 0.7 us
  other arithmetic: 11.7 us -> 0 us
    psum x2 -> x0, waiting for transfers between devices: 320 us -> none  [the longest x1 166 us: from_root(): return lax.psum(kept, axis)]
    reduce_scatter x4 -> x0, waiting for transfers between devices: 168 us -> none  [on_device(): summed = lax.psum_scatter(product, 'col', scatter_dimension=1, tiled=True)]
    all_gather x7 -> x0, blocking collectives: 124 us -> none  [the longest x4 71.5 us: on_device(): wide_panel = lax.all_gather(masked, 'col', axis=1, tiled=True)]
    all_gather x3 -> x0, waiting for transfers between devices: 122 us -> none  [on_device(): prev_block = lax.all_gather(block_local, 'col', axis=1, tiled=True)]
    pallas_call x0 -> x1, Pallas kernels: none -> 115 us  [on_device(): pl.pallas_call(functools.partial(kernel, ny), out_shape=(jax.ShapeDtypeSt...]
    dot_general x20 -> x0, matrix products: 27.9 us -> none  [the longest x4 7.11 us: on_device(): jnp.dot(trail_inverse, col_panel, preferred_element_type=jnp.float32)]
  transfers between devices with their start and end apart: 9 -> 0, of which waited for: 9 -> 0; matrix products, arithmetic and copies ran while one was open for 2% -> 0% of each run, Pallas kernels for 0% -> 0%
where the time goes in v1:
time: 124 us
  Pallas kernels  115 us (93%)
  local copies, waits for them, and re-layouts  7.57 us (6%)
    pallas_call x1, Pallas kernels, on_device(): pl.pallas_call(functools.partial(kernel, ny), out_shape=(jax.ShapeDtypeSt...  115 us
    unnamed x10, local copies, waits for them, and re-layouts  4.54 us
    pallas_call x2, local copies, waits for them, and re-layouts, on_device(): pl.pallas_call(functools.partial(kernel, ny), out_shape=(jax.ShapeDtypeSt...  3.03 us

profile of v1, /device:TPU:1, one launch (start us, length us, event | category | flops | bytes accessed | tf_op | source)
XLA Modules:
  0.0 123.6 jit_solution(7701051987545690947)
XLA Ops:
  0.6 0.0 copy-start.3
  0.6 0.0 copy-start
  0.7 1.2 copy.7.panels_ref
  1.9 1.3 %copy.8.diag_ref = f32[4,512,32]{2,1,0:T(8,128)S(1)} copy(f32[4,512,32]{1,2,0:T(8,128)} %param.8) | data formatting | bytes 524288 | tf_op args[3]
  3.2 0.0 copy-done.3
  3.2 0.0 copy-done
  3.2 0.0 copy-start.2
  3.2 1.1 copy-done.2
  4.3 115.3 %chain.1 = (bf16[4,384,32]{2,1,0:T(8,128)(2,1)S(1)}, f32[4,512,32]{2,1,0:T(8,128)S(1)}) custom-call(bf16[4,384,32]{2,1,0:T(8,128)(2,1)S(1)} %copy.7.panels_ref, s32[1,64]{1,0:T(1,128)S(1)} %bitcast.1, bf16[384,768]{1,0:T(8,128)(2,1)S(1)} %copy-done.2, bf16[3,512,512]{2,1,0:T(8,128)(2,1)S(1)} %copy-done, f32[4,512,32]{2,1,0:T(8,128)S(1)} %copy.8.diag_ref), custom_call_target="tpu_custom_call" | custom-call | tf_op jit(solution)/shard_map/chain/pallas_call | solution.py:437
  119.6 0.0 copy-start.1
  119.6 1.0 copy-done.1
  120.5 0.8 copy.9
  121.3 2.2 %copy.10 = f32[4,512,32]{1,2,0:T(8,128)} copy(f32[4,512,32]{2,1,0:T(8,128)} %copy-done.1) | data formatting | bytes 524288 | tf_op jit(solution)/shard_map/chain/pallas_call | solution.py:437
Async XLA Ops:
  0.6 2.6 %copy-start.3 = (s32[64]{0:T(128)S(1)}, s32[64]{0:T(128)}, u32[]{:S(2)}) copy-start(s32[64]{0:T(128)} %param.9) | copy-start | bytes 772
  0.6 2.6 %copy-start = (bf16[3,512,512]{2,1,0:T(8,128)(2,1)S(1)}, bf16[3,512,512]{2,1,0:T(8,128)(2,1)}, u32[]{:S(2)}) copy-start(bf16[3,512,512]{2,1,0:T(8,128)(2,1)} %coup_ref.1) | copy-start | bytes 4718596
  3.2 1.1 copy-start.2
  119.6 1.0 copy-start.1

commit v2 on v1

--- a/solution.py
+++ b/solution.py
@@ -11,7 +11,7 @@
 NX = 4
 ROWS = 384
 PIECE = 128
-LAG = 2
+LAG = 3
 MESH = pl.DeviceIdType.MESH
 F32 = jnp.float32
 BF16 = jnp.bfloat16
@@ -24,7 +24,8 @@
 
 
 def mod(value, size):
-    return lax.rem(value + 2 * size, size)
+    value = jnp.where(value < 0, value + size, value)
+    return jnp.where(value >= size, value - size, value)
 
 
 def swap_halves(value):
@@ -35,8 +36,8 @@
     ny,
     panels_ref, listed_ref, trail_ref, coup_ref, diag_ref,
     outp_ref, outd_ref,
-    tp, cc, ct, vst, dgo, dgs, dgw, mw, ms, sp, rb, ss, zs, zb, zo, ps, pb, ev, eb1, eb2, fb,
-    sem, zrecv, xrecv,
+    tp, cc, ct, vst, dgo, dgs, mw, ms, sp, rb, ss, zs, zb, zo, ps, pb, ev, eb1, eb2, fb,
+    sem, zrecv, xrecv, yrecv,
 ):
     nz = ny
     width = 64 * ny
@@ -59,40 +60,33 @@
     def wait_bytes(ref, semaphore):
         pltpu.make_async_copy(ref, ref, semaphore).wait()
 
-    (s_t, r_t, s_z, s_x, s_mw, r_mw, s_tp, r_tp, s_rs, r_rs, s_ss, r_ss, s_zb, r_zb,
+    (s_t, r_t, s_z, s_x, s_mw, r_x2, s_xh, s_tp, r_tp, s_rs, r_rs, s_ss, r_ss, s_zb, r_zb,
      s_mf, r_mf, s_zo, r_zo, s_p, r_p, s_e, r_e1, r_e2, s_f, r_f, s_dg, r_dg,
-     l_tp, l_cc, l_dg) = [sem.at[i] for i in range(30)]
+     l_tp, l_cc, l_dg) = [sem.at[i] for i in range(31)]
 
     barrier = pltpu.get_barrier_semaphore()
 
     def greet(device):
         pl.semaphore_signal(barrier, inc=1, device_id=device, device_id_type=MESH)
 
-    @pl.loop(1, 2 * ny)
-    def _(step):
-        greet((row, mod(col + step, 2 * ny)))
-
-    @pl.loop(1, NX * nz)
-    def _(step):
-        greet((mod(row + step, NX * nz), col))
+    greet(dev(x, y, z, sibling))
+    for step in (1, nz - 1) if nz > 2 else (1,):
+        greet(dev(x, y, mod(z + step, nz), h))
+    for step in range(1, NX):
+        greet(dev(mod(x + step, NX), y, z, h))
+    for step in range(1, ny):
+        greet(dev(x, mod(y + step, ny), z, h))
 
     @pl.when(y != z)
     def _():
         greet(dev(x, z, y, h))
-
-    @pl.loop(0, nz)
-    def _(zz):
-        me = jnp.logical_and(jnp.logical_and(z == y, zz == z), h == 1)
-
-        @pl.when(jnp.logical_not(me))
-        def _():
-            greet(dev(x, z, zz, 1))
 
     own_tp = pltpu.make_async_copy(trail_ref, tp.at[h], l_tp)
     own_tp.start()
     own_cc = pltpu.make_async_copy(coup_ref, cc, l_cc)
     own_cc.start()
-    own_dg = pltpu.make_async_copy(diag_ref.at[x, pl.ds(64 * z, 64)], dgo, l_dg)
+    diag_tile = diag_ref.at[x, :, pl.ds(pl.multiple_of(lax.div(z, 2) * 128, 128), 128)]
+    own_dg = pltpu.make_async_copy(diag_tile, dgo, l_dg)
     own_dg.start()
 
     listed = listed_ref[...]
@@ -104,15 +98,12 @@
     piece_mask = jnp.where(
         lane < 128, flag(3 * row), jnp.where(lane < 256, flag(3 * row + 1), flag(3 * row + 2))
     )
-    eye = jnp.where(iota((32, 32), 0) == iota((32, 32), 1), 1.0, 0.0).astype(BF16)
     for k in range(SUPER):
-        turned = lax.dot_general(eye, panels_ref[k], NT_DIMS, preferred_element_type=F32)
+        turned = panels_ref[k].astype(F32)
         mw[h, y, 32 * k:32 * (k + 1), :] = (turned * piece_mask).astype(BF16)
 
-    off_diagonal = jnp.where(y != z, 1, 0)
     pl.semaphore_wait(
-        barrier,
-        (2 * ny - 1) + (NX * nz - 1) + off_diagonal + h * (2 * ny - 1 + off_diagonal),
+        barrier, min(2, nz - 1) + NX + ny - 1 + jnp.where(y != z, 1, 0)
     )
 
     mine = mw.at[h, y]
@@ -127,9 +118,7 @@
 
     send_tp = remote(trail_ref, tp.at[h], s_tp, r_tp, dev(x, y, z, sibling))
     send_tp.start()
-    send_dg = remote(
-        diag_ref.at[x, pl.ds(64 * z, 64)], dgs, s_dg, r_dg, dev(x, y, z, sibling)
-    )
+    send_dg = remote(diag_tile, dgs, s_dg, r_dg, dev(x, y, z, sibling))
     send_dg.start()
 
     def near(step):
@@ -137,16 +126,8 @@
         return jnp.where(lax.rem(step, 2) == 1, half, mod(-half, nz))
 
     home = ms.at[z * NX + x]
+    right, left = dev(mod(x + 1, NX), y, z, h), dev(mod(x - 1, NX), y, z, h)
     wait_bytes(home, r_t)
-
-    @pl.loop(1, nz)
-    def _(step):
-        delta = near(step)
-        remote(home, home, s_z, zrecv.at[delta], dev(x, y, mod(z + delta, nz), h)).start()
-
-    @pl.loop(1, ny)
-    def _(step):
-        remote(mine, mine, s_mw, r_mw, dev(x, mod(y + near(step), ny), z, h)).start()
 
     own_tp.wait()
     wait_bytes(tp.at[0], r_tp)
@@ -157,21 +138,53 @@
         def _():
             delta = near(step)
             slot = ms.at[mod(z - delta, nz) * NX + x]
+            wide = mw.at[h, mod(y - delta, ny)]
+            ahead = lax.rem(step, 2) == 1
+            z_next = mod(z + jnp.where(ahead, 1, -1), nz)
+            y_next = mod(y + jnp.where(ahead, 1, -1), ny)
 
             @pl.when(step > 0)
             def _():
-                wait_bytes(slot, zrecv.at[delta])
-
-            for dx in (1, 3, 2):
-                remote(
-                    slot, slot, s_x, xrecv.at[delta], dev(mod(x + dx, NX), y, z, h)
-                ).start()
+                wait_bytes(slot, zrecv.at[step])
+
+            @pl.when(step == 0)
+            def _():
+                remote(slot, slot, s_z, zrecv.at[1], dev(x, y, mod(z + 1, nz), h)).start()
+
+            @pl.when(step < nz - 2)
+            def _():
+                remote(slot, slot, s_z, zrecv.at[step + 2], dev(x, y, z_next, h)).start()
+
+            remote(slot, slot, s_x, xrecv.at[0, step], right).start()
+            remote(slot, slot, s_x, xrecv.at[1, step], left).start()
+
+            @pl.when(step > 0)
+            def _():
+                wait_bytes(wide, yrecv.at[step])
+
+            @pl.when(step == 0)
+            def _():
+                remote(wide, wide, s_mw, yrecv.at[1], dev(x, mod(y + 1, ny), z, h)).start()
+
+            @pl.when(step < ny - 2)
+            def _():
+                remote(wide, wide, s_mw, yrecv.at[step + 2], dev(x, y_next, z, h)).start()
+
+        @pl.when(jnp.logical_and(step >= 1, step <= nz))
+        def _():
+            at = step - 1
+            first = mod(z - near(at), nz) * NX
+            for way, source, to, rows in ((0, x - 1, right, 0), (1, x + 1, left, 64)):
+                slot = ms.at[first + mod(source, NX)]
+                wait_bytes(slot, xrecv.at[way, at])
+                half = slot.at[pl.ds(rows, 64)]
+                remote(half, half, s_xh, xrecv.at[2, at], to).start()
 
         @pl.when(step >= LAG)
         def _():
-            delta = near(step - LAG)
-            chunk = mod(z - delta, nz)
-            wait_bytes(ms.at[pl.ds(0, NX - 1)], xrecv.at[delta])
+            at = step - LAG
+            chunk = mod(z - near(at), nz)
+            wait_bytes(home, xrecv.at[2, at])
             total = None
             for xx in range(NX):
                 term = lax.dot_general(
@@ -184,8 +197,7 @@
             for yy in range(ny):
                 sp[yy, :, lanes] = total[chain_rows * yy:chain_rows * (yy + 1)]
 
-            @pl.loop(1, ny)
-            def _(i):
+            for i in range(1, ny):
                 to = mod(y + i, ny)
                 remote(
                     sp.at[to, :, lanes], rb.at[i - 1, :, lanes], s_rs, r_rs, dev(x, to, z, h)
@@ -210,13 +222,10 @@
 
     own_dg.wait()
     wait_bytes(dgs, r_dg)
-    dgw[...] = jnp.zeros_like(dgw)
-    dgw[0, :, 0:32] = dgo[...]
-    dgw[1, :, 0:32] = dgs[...]
-    both = dgw[0] + pltpu.roll(dgw[1], 32, 1)
-    diag_packed = both[0:32] + swap_halves(both[32:64])
-
-    wait_bytes(mw.at[0, pl.ds(0, ny - 1)], r_mw)
+    both = jnp.concatenate([dgo[...], dgs[...], jnp.zeros((64, 128), F32)], axis=0)
+    both = jnp.where(lax.rem(z, 2) == 0, both, swap_halves(both)).T
+    diag_packed = jnp.where(iota((32, 128), 1) < 64, both[0:32], swap_halves(both[32:64]))
+
     send_mf = remote(mw.at[h], mw.at[h], s_mf, r_mf, dev(x, y, z, sibling))
     send_mf.start()
 
@@ -268,8 +277,7 @@
 
     own_rows = pl.ds(pl.multiple_of(chain_rows * y, 16), chain_rows)
 
-    @pl.loop(1, ny)
-    def _(i):
+    for i in range(1, ny):
         to = mod(y + i, ny)
         remote(zs.at[to], zb.at[own_rows], s_zb, r_zb, dev(x, to, z, h)).start()
 
@@ -299,26 +307,25 @@
                 packed = jnp.where(low32, swap_halves(upper), lower)
             ps[k * nz + zz] = packed.astype(BF16)
 
-    @pl.loop(1, NX * nz)
-    def _(i):
-        xx = mod(x + lax.div(i, nz), NX)
-        zz = mod(z + lax.rem(i, nz), nz)
+    for i in range(1, NX * nz):
+        xx, zz = mod(x + i // nz, NX), mod(z + i % nz, nz)
         remote(ps.at[xx * nz + zz], pb.at[i - 1], s_p, r_p, dev(xx, y, zz, h)).start()
 
+    own_lane = 64 * lax.div(iota((128, 256), 0), 32) + 32 * h + lax.rem(iota((128, 256), 0), 32)
+    own_lane = jnp.where(iota((128, 256), 1) == own_lane, 1.0, 0.0).astype(BF16)
+
+    def write_panel(source):
+        turned = lax.dot_general(own_lane, source[...], NT_DIMS, preferred_element_type=F32)
+        outp_ref[...] = turned.astype(BF16).reshape(SUPER, 32, ROWS)
+
     @pl.when(h == 0)
     def _():
-        for k in range(SUPER):
-            tile = zb[:, 128 * (k // 2):128 * (k // 2 + 1)].astype(F32)
-            tile = swap_halves(tile) if k % 2 else tile
-            outp_ref[k] = tile[:, 0:32].astype(BF16)
+        write_panel(zb)
 
     @pl.when(h == 1)
     def _():
         wait_bytes(zo, r_zo)
-        for k in range(SUPER):
-            tile = zo[:, 128 * (k // 2):128 * (k // 2 + 1)].astype(F32)
-            tile = pltpu.roll(tile, 32 if k % 2 else 96, 1)
-            outp_ref[k] = tile[:, 0:32].astype(BF16)
+        write_panel(zo)
 
     wait_bytes(pb, r_p)
     total = ps[x * nz + z].astype(F32)
@@ -326,31 +333,27 @@
         total = total + pb[i].astype(F32)
     ev[...] = jnp.where(h == 0, diag_packed - total, total).astype(BF16)
 
-    @pl.loop(0, 2 * ny)
-    def _(i):
-        yy, hh = lax.div(i, 2), lax.rem(i, 2)
-
-        @pl.when(h == 0)
-        def _():
-            @pl.when(i == col)
-            def _():
-                pltpu.make_async_copy(ev, eb1.at[y], r_e1).start()
-
-            @pl.when(i != col)
-            def _():
-                remote(ev, eb1.at[y], s_e, r_e1, dev(x, yy, z, hh)).start()
-
-        @pl.when(h == 1)
-        def _():
-            me = jnp.logical_and(i == col, y == z)
-
-            @pl.when(me)
-            def _():
-                pltpu.make_async_copy(ev, eb2.at[z], r_e2).start()
-
-            @pl.when(jnp.logical_not(me))
-            def _():
-                remote(ev, eb2.at[z], s_e, r_e2, dev(x, yy, y, hh)).start()
+    @pl.when(h == 0)
+    def _():
+        pltpu.make_async_copy(ev, eb1.at[y], r_e1).start()
+        for i in range(1, 2 * ny):
+            yy = mod(y + i // 2, ny)
+            remote(ev, eb1.at[y], s_e, r_e1, dev(x, yy, z, i % 2)).start()
+
+    @pl.when(h == 1)
+    def _():
+        for i in range(2 * ny):
+            yy = mod(y + i // 2, ny)
+            if i == 1:
+                @pl.when(y == z)
+                def _():
+                    pltpu.make_async_copy(ev, eb2.at[z], r_e2).start()
+
+                @pl.when(y != z)
+                def _():
+                    remote(ev, eb2.at[z], s_e, r_e2, dev(x, yy, y, 1)).start()
+            else:
+                remote(ev, eb2.at[z], s_e, r_e2, dev(x, yy, y, i % 2)).start()
 
     wait_bytes(eb1, r_e1)
     wait_bytes(eb2, r_e2)
@@ -375,14 +378,13 @@
     own = jnp.dot(straight, right, preferred_element_type=F32) + turned[0:64]
     mine_f = fb.at[x * nz + z]
     mine_f[...] = own.astype(BF16)
-
-    @pl.loop(1, NX * nz)
-    def _(i):
-        xx = mod(x + lax.div(i, nz), NX)
-        zz = mod(z + lax.rem(i, nz), nz)
-        remote(mine_f, mine_f, s_f, r_f, dev(xx, y, zz, h)).start()
-
-    wait_bytes(fb.at[pl.ds(0, NX * nz - 1)], r_f)
+    for i in range(1, nz):
+        remote(mine_f, mine_f, s_f, r_f, dev(x, y, mod(z + i, nz), h)).start()
+    wait_bytes(fb.at[pl.ds(0, nz - 1)], r_f)
+    mine_x = fb.at[pl.ds(pl.multiple_of(x * nz, nz), nz)]
+    for i in (1, 3, 2):
+        remote(mine_x, mine_x, s_f, r_x2, dev(mod(x + i, NX), y, z, h)).start()
+    wait_bytes(fb.at[pl.ds(0, (NX - 1) * nz)], r_x2)
     state = fb[pl.ds(0, nz)].reshape(width, 128).astype(F32)
     for j in range(SUPER - 1):
         high = state.astype(BF16)
@@ -393,8 +395,7 @@
         moved = moved[:, 0:128] + moved[:, 128:256]
         added = fb[pl.ds((j + 1) * nz, nz)].reshape(width, 128).astype(F32)
         state = added + jnp.where(group > j, moved, state)
-    for k in range(SUPER):
-        outd_ref[k] = (pltpu.roll(state, 128 - 32 * k, 1) if k else state)[:, 0:32]
+    outd_ref[...] = state.T.reshape(SUPER, 32, width)
 
     @pl.when(y != z)
     def _():
@@ -404,7 +405,8 @@
     wait_bytes(dgs, s_dg)
     wait_bytes(ms.at[pl.ds(0, nz - 1)], s_z)
     wait_bytes(mw.at[0, pl.ds(0, ny - 1)], s_mw)
-    wait_bytes(ms.at[pl.ds(0, (NX - 1) * nz)], s_x)
+    wait_bytes(ms.at[pl.ds(0, 2 * nz)], s_x)
+    wait_bytes(ms.at[pl.ds(0, nz)], s_xh)
     wait_bytes(rb, s_rs)
     wait_bytes(mw.at[0], s_mf)
     wait_bytes(ss.at[0], s_ss)
@@ -424,7 +426,8 @@
     def _():
         wait_bytes(ev, s_e)
 
-    wait_bytes(fb.at[pl.ds(0, NX * nz - 1)], s_f)
+    wait_bytes(fb.at[pl.ds(0, nz - 1)], s_f)
+    wait_bytes(fb.at[pl.ds(0, (NX - 1) * nz)], s_f)
 
 
 def on_device(trail_inverse, panels, couplings, diag_terms, listed):
@@ -434,11 +437,11 @@
     chain_rows = ROWS // ny
     vmem = pl.BlockSpec(memory_space=pltpu.VMEM)
     anywhere = pl.BlockSpec(memory_space=pl.ANY)
-    return pl.pallas_call(
+    panel, diag = pl.pallas_call(
         functools.partial(kernel, ny),
         out_shape=(
-            jax.ShapeDtypeStruct((SUPER, ROWS, 32), BF16),
-            jax.ShapeDtypeStruct((SUPER, width, 32), F32),
+            jax.ShapeDtypeStruct((SUPER, 32, ROWS), BF16),
+            jax.ShapeDtypeStruct((SUPER, 32, width), F32),
         ),
         in_specs=[vmem, vmem, anywhere, anywhere, anywhere],
         out_specs=(vmem, vmem),
@@ -447,9 +450,8 @@
             pltpu.VMEM((SUPER - 1, width, width), BF16),
             pltpu.VMEM((SUPER - 1, width, width), BF16),
             pltpu.VMEM((SUPER, width, 128), BF16),
-            pltpu.VMEM((64, 32), F32),
-            pltpu.VMEM((64, 32), F32),
-            pltpu.VMEM((2, 64, 128), F32),
+            pltpu.VMEM((32, 128), F32),
+            pltpu.VMEM((32, 128), F32),
             pltpu.VMEM((2, ny, PIECE, ROWS), BF16),
             pltpu.VMEM((nz * NX, PIECE, ROWS), BF16),
             pltpu.VMEM((ny, chain_rows, 128 * ny), BF16),
@@ -464,15 +466,20 @@
             pltpu.VMEM((ny, 32, 128), BF16),
             pltpu.VMEM((nz, 32, 128), BF16),
             pltpu.VMEM((NX * nz, 64, 128), BF16),
-            pltpu.SemaphoreType.DMA((30,)),
+            pltpu.SemaphoreType.DMA((31,)),
             pltpu.SemaphoreType.DMA((nz,)),
-            pltpu.SemaphoreType.DMA((nz,)),
+            pltpu.SemaphoreType.DMA((3, nz)),
+            pltpu.SemaphoreType.DMA((ny,)),
         ],
         compiler_params=pltpu.CompilerParams(
-            collective_id=0, has_side_effects=True, vmem_limit_bytes=48 * 1024 * 1024
+            collective_id=0, has_side_effects=True, vmem_limit_bytes=60 * 1024 * 1024
         ),
         name="chain",
-    )(panels, listed.reshape(1, -1), trail_inverse, couplings, diag_terms)
+    )(
+        panels.swapaxes(1, 2), listed.reshape(1, -1), trail_inverse, couplings,
+        diag_terms.swapaxes(1, 2),
+    )
+    return panel.swapaxes(1, 2), diag.swapaxes(1, 2)
 
 
 def solution(mesh):

time: 124 us -> 109 us (0.88)
  Pallas kernels: 115 us -> 104 us
  local copies, waits for them, and re-layouts: 7.57 us -> 3.21 us
    pallas_call x1, Pallas kernels: 115 us -> 104 us  [on_device(): pl.pallas_call(functools.partial(kernel, ny), out_shape=(jax.ShapeDtypeSt...]
    pallas_call x2 -> x0, local copies, waits for them, and re-layouts: 3.03 us -> none  [on_device(): pl.pallas_call(functools.partial(kernel, ny), out_shape=(jax.ShapeDtypeSt...]
    unnamed x10 -> x2, local copies, waits for them, and re-layouts: 4.54 us -> 3.21 us
where the time goes in v2:
time: 109 us; the launch traced here: 108 us
  Pallas kernels  104 us (95%)
  local copies, waits for them, and re-layouts  3.21 us (3%)
    pallas_call x1, Pallas kernels, on_device(): pl.pallas_call(functools.partial(kernel, ny), out_shape=(jax.ShapeDtypeSt...  104 us
    unnamed x2, local copies, waits for them, and re-layouts  3.21 us

profile of v2, /device:TPU:1, one launch (start us, length us, event | category | flops | bytes accessed | tf_op | source)
XLA Modules:
  0.0 108.2 jit_solution(4193722910178246781)
XLA Ops:
  0.6 104.4 %chain.1 = (bf16[4,32,384]{2,1,0:T(8,128)(2,1)}, f32[4,32,512]{2,1,0:T(8,128)}) custom-call(bf16[4,32,384]{2,1,0:T(8,128)(2,1)} %bitcast.7, s32[1,64]{1,0:T(1,128)} %bitcast.9, bf16[384,768]{1,0:T(8,128)(2,1)} %trail_ref.1, bf16[3,512,512]{2,1,0:T(8,128)(2,1)} %coup_ref.1, f32[4,32,512]{2,1,0:T(8,128)} %bitcast.6), custom_call_target="tpu_custom_call" | custom-call | tf_op jit(solution)/shard_map/chain/pallas_call | solution.py:440
  105.0 1.5 %copy.9 = bf16[4,384,32]{1,2,0:T(8,128)(2,1)} copy(bf16[4,384,32]{1,2,0:T(8,128)(2,1)} %bitcast.8) | data formatting | bytes 196608
  106.6 1.7 %copy.10 = f32[4,512,32]{1,2,0:T(8,128)} copy(f32[4,512,32]{1,2,0:T(8,128)} %bitcast.5) | data formatting | bytes 524288

commit v3 on v2

v3 whole, which is shorter than its diff:
```python
import functools

import jax
import jax.numpy as jnp
from jax import lax
from jax.experimental import pallas as pl
from jax.experimental.pallas import tpu as pltpu
from jax.sharding import PartitionSpec as P

SUPER = 4
NX = 4
ROWS = 384
PIECE = 128
LAG = 3
ADD = 5
MESH = pl.DeviceIdType.MESH
F32 = jnp.float32
BF16 = jnp.bfloat16
NT_DIMS = (((1,), (1,)), ((), ()))
TN_DIMS = (((0,), (0,)), ((), ()))


def iota(shape, dim):
    return lax.broadcasted_iota(jnp.int32, shape, dim)


def mod(value, size):
    value = jnp.where(value < 0, value + size, value)
    return jnp.where(value >= size, value - size, value)


def split(value):
    high = value.astype(BF16)
    return [high, (value - high.astype(F32)).astype(BF16)]


def swap_halves(value):
    return pltpu.roll(value, 64, 1)


def kernel(
    ny,
    panels_ref, listed_ref, trail_ref, coup_ref, diag_ref,
    outp_ref, outd_ref,
    tp, cc, ct, vst, dgo, dgs, mw, ms, part, out, got, sp, rb, ss, zs, zb, zo, ps, pb, ev, eb1, eb2, fb,
    sem, zrecv, xrecv, precv, yrecv, frecv,
):
    nz = ny
    width = 64 * ny
    chain_rows = ROWS // ny
    tiles = width // 128
    row, col = lax.axis_index("row"), lax.axis_index("col")
    z, x = lax.div(row, NX), lax.rem(row, NX)
    y, h = lax.div(col, 2), lax.rem(col, 2)
    sibling = 1 - h

    def dev(xx, yy, zz, hh):
        return (zz * NX + xx, yy * 2 + hh)

    def remote(src, dst, send, recv, device):
        return pltpu.make_async_remote_copy(
            src_ref=src, dst_ref=dst, send_sem=send, recv_sem=recv,
            device_id=device, device_id_type=MESH,
        )

    def wait_bytes(ref, semaphore):
        pltpu.make_async_copy(ref, ref, semaphore).wait()

    (s_t, r_t, s_z, s_x, s_mw, s_p2, r_t2, s_eb, s_td, r_td, s_tp, r_tp, s_rs, r_rs, s_ss, r_ss, s_zb, r_zb,
     s_mf, r_mf, s_zo, r_zo, s_p, r_p, s_e, r_e1, r_e2, s_f, r_f, s_dg, r_dg,
     l_tp, l_cc, l_dg) = [sem.at[i] for i in range(34)]

    barrier = pltpu.get_barrier_semaphore()

    def greet(device):
        pl.semaphore_signal(barrier, inc=1, device_id=device, device_id_type=MESH)

    greet(dev(x, y, z, sibling))
    for step in (1, nz - 1) if nz > 2 else (1,):
        greet(dev(x, y, mod(z + step, nz), h))
    for step in range(1, NX):
        greet(dev(mod(x + step, NX), y, z, h))
    for step in range(1, ny):
        greet(dev(x, mod(y + step, ny), z, h))

    @pl.when(y != z)
    def _():
        greet(dev(x, z, y, h))

    pair = x + 1 - 2 * lax.rem(x, 2)
    inner = jnp.where(jnp.logical_or(x == 1, x == 2), 1, 0)

    def side_of(core):
        return jnp.where(core == inner, 0, 1)

    kept_side, given_side = side_of(h), 1 - side_of(h)
    own_tp = pltpu.make_async_copy(
        trail_ref.at[:, pl.ds(pl.multiple_of(kept_side * ROWS, ROWS), ROWS)], tp.at[h, 0], l_tp
    )
    own_tp.start()
    own_cc = pltpu.make_async_copy(coup_ref, cc, l_cc)
    own_cc.start()
    diag_tile = diag_ref.at[x, :, pl.ds(pl.multiple_of(lax.div(z, 2) * 128, 128), 128)]
    own_dg = pltpu.make_async_copy(diag_tile, dgo, l_dg)
    own_dg.start()

    listed = listed_ref[...]

    def flag(block):
        return jnp.max(jnp.where(listed == block, 1.0, 0.0), axis=1, keepdims=True)

    lane = iota((1, ROWS), 1)
    piece_mask = jnp.where(
        lane < 128, flag(3 * row), jnp.where(lane < 256, flag(3 * row + 1), flag(3 * row + 2))
    )
    for k in range(SUPER):
        turned = panels_ref[k].astype(F32)
        mw[h, y, 32 * k:32 * (k + 1), :] = (turned * piece_mask).astype(BF16)

    pl.semaphore_wait(
        barrier, min(2, nz - 1) + NX + ny - 1 + jnp.where(y != z, 1, 0)
    )

    mine = mw.at[h, y]
    landed = (r_t, r_t2)
    halves = [pl.ds(64 * half, 64) for half in range(2)]

    for half in range(2):
        target = ms.at[y * NX + x, halves[half]]

        @pl.when(y != z)
        def _():
            remote(mine.at[halves[half]], target, s_t, landed[half], dev(x, z, y, h)).start()

        @pl.when(y == z)
        def _():
            pltpu.make_async_copy(mine.at[halves[half]], target, landed[half]).start()

    given = trail_ref.at[:, pl.ds(pl.multiple_of(given_side * ROWS, ROWS), ROWS)]
    remote(given, tp.at[h, 1], s_tp, r_tp, dev(pair, y, z, h)).start()
    send_dg = remote(diag_tile, dgs, s_dg, r_dg, dev(x, y, z, sibling))
    send_dg.start()

    def near(step):
        half = lax.div(step + 1, 2)
        return jnp.where(lax.rem(step, 2) == 1, half, mod(-half, nz))

    home = ms.at[z * NX + x]
    own_cc.wait()
    wide_eye = jnp.where(iota((width, width), 0) == iota((width, width), 1), 1.0, 0.0)
    wide_eye = wide_eye.astype(BF16)
    group = lax.div(iota((width, 128), 1), 32)
    picks = iota((width, 128), 0) == col * 32 + lax.rem(iota((width, 128), 1), 32)
    for j in range(SUPER - 1):
        ct[j] = lax.dot_general(
            wide_eye, cc[j], NT_DIMS, preferred_element_type=F32
        ).astype(BF16)
    above = None
    for j in reversed(range(SUPER)):
        chosen = jnp.where(jnp.logical_and(picks, group == j), 1.0, 0.0)
        if above is not None:
            chosen = chosen + jnp.dot(cc[j], above, preferred_element_type=F32)
        above = chosen.astype(BF16)
        vst[j] = above

    own_dg.wait()
    wait_bytes(dgs, r_dg)
    both = jnp.concatenate([dgo[...], dgs[...], jnp.zeros((64, 128), F32)], axis=0)
    both = jnp.where(lax.rem(z, 2) == 0, both, swap_halves(both)).T
    diag_packed = jnp.where(iota((32, 128), 1) < 64, both[0:32], swap_halves(both[32:64]))

    own_tp.wait()
    wait_bytes(tp.at[0, 0], r_tp)
    remote(tp.at[h], tp.at[h], s_td, r_td, dev(x, y, z, sibling)).start()
    wait_bytes(tp.at[0], r_td)

    def relay_piece(step, half):
        slot = ms.at[mod(z - near(step), nz) * NX + x, halves[half]]
        z_next = mod(z + jnp.where(lax.rem(step, 2) == 1, 1, -1), nz)

        @pl.when(step > 0)
        def _():
            wait_bytes(slot, zrecv.at[half, step])

        @pl.when(step == 0)
        def _():
            wait_bytes(slot, landed[half])
            remote(slot, slot, s_z, zrecv.at[half, 1], dev(x, y, mod(z + 1, nz), h)).start()

        @pl.when(step < nz - 2)
        def _():
            remote(slot, slot, s_z, zrecv.at[half, step + 2], dev(x, y, z_next, h)).start()

        remote(slot, slot, s_x, xrecv.at[half, step], dev(3 - x, y, z, h)).start()

    def relay_wide(step):
        wide = mw.at[h, mod(y - near(step), ny)]
        y_next = mod(y + jnp.where(lax.rem(step, 2) == 1, 1, -1), ny)

        @pl.when(step > 0)
        def _():
            wait_bytes(wide, yrecv.at[step])

        @pl.when(step == 0)
        def _():
            remote(wide, wide, s_mw, yrecv.at[1], dev(x, mod(y + 1, ny), z, h)).start()

        @pl.when(step < ny - 2)
        def _():
            remote(wide, wide, s_mw, yrecv.at[step + 2], dev(x, y_next, z, h)).start()

    @pl.loop(0, nz + ADD)
    def _(step):
        @pl.when(step < nz)
        def _():
            relay_piece(step, 0)

        @pl.when(jnp.logical_and(step >= 1, step <= nz))
        def _():
            relay_piece(step - 1, 1)

        @pl.when(step < nz)
        def _():
            relay_wide(step)

        @pl.when(jnp.logical_and(step >= LAG, step < nz + LAG))
        def _():
            at = step - LAG
            chunk = mod(z - near(at), nz)
            for half in range(2):
                wait_bytes(home.at[halves[half]], xrecv.at[half, at])
            sums = [None, None]
            for core in range(2):
                piece = ms[chunk * NX + 2 * core + side_of(core)]
                for rows in range(2):
                    term = lax.dot_general(
                        tp[core, rows], piece, NT_DIMS, preferred_element_type=F32
                    )
                    sums[rows] = term if core == 0 else sums[rows] + term
            part[chunk] = sums[0]
            out[chunk] = sums[1].astype(BF16)
            remote(out.at[chunk], got.at[chunk], s_p2, precv.at[at], dev(pair, y, z, h)).start()

        @pl.when(step >= ADD)
        def _():
            at = step - ADD
            chunk = mod(z - near(at), nz)
            wait_bytes(got.at[chunk], precv.at[at])
            total = part[chunk] + got[chunk].astype(F32)
            total = total.astype(BF16)
            lanes = pl.ds(pl.multiple_of(chunk * PIECE, PIECE), PIECE)
            for yy in range(ny):
                sp[yy, :, lanes] = total[chain_rows * yy:chain_rows * (yy + 1)]

            for i in range(1, ny):
                to = mod(y + i, ny)
                remote(
                    sp.at[to, :, lanes], rb.at[i - 1, :, lanes], s_rs, r_rs, dev(x, to, z, h)
                ).start()

    send_mf = remote(mw.at[h], mw.at[h], s_mf, r_mf, dev(x, y, z, sibling))
    send_mf.start()

    wait_bytes(rb, r_rs)
    for t in range(ny):
        lanes = slice(128 * t, 128 * (t + 1))
        total = sp[y, :, lanes].astype(F32)
        for i in range(ny - 1):
            total = total + rb[i, :, lanes].astype(F32)
        ss[h, :, lanes] = total
    send_ss = remote(ss.at[h], ss.at[h], s_ss, r_ss, dev(x, y, z, sibling))
    send_ss.start()
    wait_bytes(ss.at[0], r_ss)

    block = lax.shift_right_logical(
        ROWS * row + chain_rows * y + iota((chain_rows, 1), 0), 7
    )
    row_mask = jnp.max(jnp.where(listed == block, 1.0, 0.0), axis=1, keepdims=True)
    quarter = lax.div(iota((chain_rows, 128), 1), 32)
    low = iota((chain_rows, 128), 1) < 64
    result = None
    kept = []
    for k in range(SUPER):
        found = []
        for t in range(tiles):
            tile = None
            for g in range(4):
                yy = 2 * t + g // 2
                source = ss[g % 2, :, 128 * yy:128 * (yy + 1)]
                shift = (32 * (g - k)) % 128
                if shift:
                    source = pltpu.roll(source, shift, 1)
                tile = source if tile is None else jnp.where(quarter == g, source, tile)
            found.append(tile)
        summed = jnp.concatenate(found, axis=1) if tiles > 1 else found[0]
        carried = jnp.zeros_like(summed)
        if k > 0:
            carried = jnp.dot(result, cc[k - 1], preferred_element_type=F32)
            summed = summed + carried
        result = (-(summed * row_mask)).astype(BF16)
        kept.append(jnp.where(h == 0, result.astype(F32), carried))
    for two in range(SUPER // 2):
        for t in range(tiles):
            tile = slice(128 * t, 128 * (t + 1))
            first, second = kept[2 * two][:, tile], kept[2 * two + 1][:, tile]
            lanes = slice(128 * two, 128 * (two + 1))
            zs[2 * t, :, lanes] = jnp.where(low, first, swap_halves(second)).astype(BF16)
            zs[2 * t + 1, :, lanes] = jnp.where(low, swap_halves(first), second).astype(BF16)

    own_rows = pl.ds(pl.multiple_of(chain_rows * y, 16), chain_rows)

    for i in range(1, ny):
        to = mod(y + i, ny)
        remote(zs.at[to], zb.at[own_rows], s_zb, r_zb, dev(x, to, z, h)).start()

    zb[own_rows, :] = zs[y]
    wait_bytes(mw.at[0], r_mf)
    wait_bytes(zb.at[pl.ds(0, chain_rows * (ny - 1))], r_zb)

    @pl.when(h == 0)
    def _():
        remote(zb, zo, s_zo, r_zo, dev(x, y, z, 1)).start()

    low32 = iota((32, 128), 1) < 64
    for k in range(SUPER):
        left = jnp.concatenate(
            [mw[c % 2, c // 2, 32 * k:32 * (k + 1), :] for c in range(2 * ny)], axis=0
        )
        two = k // 2
        product = jnp.dot(
            left, zb[:, 128 * two:128 * (two + 1)], preferred_element_type=F32
        )
        for zz in range(nz):
            upper = product[64 * zz:64 * zz + 32]
            lower = product[64 * zz + 32:64 * zz + 64]
            if k % 2 == 0:
                packed = jnp.where(low32, upper, swap_halves(lower))
            else:
                packed = jnp.where(low32, swap_halves(upper), lower)
            ps[k * nz + zz] = packed.astype(BF16)

    for i in range(1, NX * nz):
        xx, zz = mod(x + i // nz, NX), mod(z + i % nz, nz)
        remote(ps.at[xx * nz + zz], pb.at[i - 1], s_p, r_p, dev(xx, y, zz, h)).start()

    own_lane = 64 * lax.div(iota((128, 256), 0), 32) + 32 * h + lax.rem(iota((128, 256), 0), 32)
    own_lane = jnp.where(iota((128, 256), 1) == own_lane, 1.0, 0.0).astype(BF16)

    def write_panel(source):
        turned = lax.dot_general(own_lane, source[...], NT_DIMS, preferred_element_type=F32)
        outp_ref[...] = turned.astype(BF16).reshape(SUPER, 32, ROWS)

    @pl.when(h == 0)
    def _():
        write_panel(zb)

    @pl.when(h == 1)
    def _():
        wait_bytes(zo, r_zo)
        write_panel(zo)

    wait_bytes(pb, r_p)
    total = ps[x * nz + z].astype(F32)
    for i in range(NX * nz - 1):
        total = total + pb[i].astype(F32)
    ev[...] = jnp.where(h == 0, diag_packed - total, total)

    @pl.when(h == 0)
    def _():
        for i in range(1, ny):
            remote(ev, eb1.at[y], s_e, r_e1, dev(x, mod(y + i, ny), z, 0)).start()
        eb1[y] = ev[...]
        wait_bytes(eb1.at[pl.ds(0, ny - 1)], r_e1)
        remote(eb1, eb1, s_eb, r_e2, dev(x, y, z, 1)).start()

    @pl.when(h == 1)
    def _():
        for i in range(1, ny):
            remote(ev, eb2.at[z], s_e, r_e1, dev(x, mod(y + i, ny), y, 1)).start()

        @pl.when(y == z)
        def _():
            pltpu.make_async_copy(ev, eb2.at[z], r_e1).start()

        @pl.when(y != z)
        def _():
            remote(ev, eb2.at[z], s_e, r_e1, dev(x, y, y, 1)).start()

        wait_bytes(eb2, r_e1)
        remote(eb2, eb2, s_eb, r_e2, dev(x, y, z, 0)).start()

    wait_bytes(eb1, r_e2)
    upper, lower = [], []
    for t in range(tiles):
        first, second = eb1[2 * t], eb1[2 * t + 1]
        upper.append(jnp.where(low32, first, swap_halves(second)))
        lower.append(jnp.where(low32, swap_halves(first), second))
    if tiles > 1:
        upper = jnp.concatenate(upper, axis=1)
        lower = jnp.concatenate(lower, axis=1)
    else:
        upper, lower = upper[0], lower[0]
    straight = jnp.concatenate(split(jnp.concatenate([upper, lower], axis=0)), axis=0)
    stack = []
    for b in range(nz):
        stack += [eb2[b], swap_halves(eb2[b])]
    high, rest = split(jnp.concatenate(stack, axis=0))
    stack = jnp.where(
        iota((width, 128), 1) < 64, high.astype(F32), swap_halves(rest.astype(F32))
    ).astype(BF16)
    right_side = vst[x]
    own = jnp.dot(straight, right_side, preferred_element_type=F32)
    own = own + lax.dot_general(stack, right_side, TN_DIMS, preferred_element_type=F32)
    own = own[0:64] + own[64:128]
    mine_f = fb.at[x * nz + z]
    mine_f[...] = own.astype(BF16)
    order = [(i + 1) // 2 if i % 2 else nz - i // 2 for i in range(1, nz)]
    for delta in order:
        remote(mine_f, mine_f, s_f, frecv.at[delta], dev(x, y, mod(z + delta, nz), h)).start()
    for delta in [0] + order:
        slot = fb.at[x * nz + mod(z - delta, nz)]
        if delta:
            wait_bytes(slot, frecv.at[delta])
        for i in (2, 1, 3):
            remote(slot, slot, s_f, r_f, dev(mod(x + i, NX), y, z, h)).start()
    wait_bytes(fb.at[pl.ds(0, (NX - 1) * nz)], r_f)
    state = fb[pl.ds(0, nz)].reshape(width, 128).astype(F32)
    for j in range(SUPER - 1):
        moved = jnp.dot(
            ct[j], jnp.concatenate(split(state), axis=1), preferred_element_type=F32
        )
        moved = moved[:, 0:128] + moved[:, 128:256]
        added = fb[pl.ds((j + 1) * nz, nz)].reshape(width, 128).astype(F32)
        state = added + jnp.where(group > j, moved, state)
    outd_ref[...] = state.T.reshape(SUPER, 32, width)

    @pl.when(y != z)
    def _():
        wait_bytes(home, s_t)

    wait_bytes(tp.at[0, 0], s_tp)
    wait_bytes(tp.at[0], s_td)
    wait_bytes(dgs, s_dg)
    wait_bytes(ms.at[pl.ds(0, nz - 1)], s_z)
    wait_bytes(mw.at[0, pl.ds(0, ny - 1)], s_mw)
    wait_bytes(ms.at[pl.ds(0, nz)], s_x)
    wait_bytes(got, s_p2)
    wait_bytes(rb, s_rs)
    wait_bytes(mw.at[0], s_mf)
    wait_bytes(ss.at[0], s_ss)
    wait_bytes(zb.at[pl.ds(0, chain_rows * (ny - 1))], s_zb)

    @pl.when(h == 0)
    def _():
        wait_bytes(zo, s_zo)

    wait_bytes(pb, s_p)
    wait_bytes(eb1.at[pl.ds(0, ny - 1)], s_e)
    wait_bytes(eb1, s_eb)

    @pl.when(jnp.logical_and(h == 1, y != z))
    def _():
        wait_bytes(ev, s_e)

    wait_bytes(fb.at[pl.ds(0, nz - 1)], s_f)
    wait_bytes(fb.at[pl.ds(0, (NX - 1) * nz)], s_f)


def on_device(trail_inverse, panels, couplings, diag_terms, listed):
    ny = lax.axis_size("col") // 2
    nz = ny
    width = 64 * ny
    chain_rows = ROWS // ny
    vmem = pl.BlockSpec(memory_space=pltpu.VMEM)
    anywhere = pl.BlockSpec(memory_space=pltpu.HBM)
    panel, diag = pl.pallas_call(
        functools.partial(kernel, ny),
        out_shape=(
            jax.ShapeDtypeStruct((SUPER, 32, ROWS), BF16),
            jax.ShapeDtypeStruct((SUPER, 32, width), F32),
        ),
        in_specs=[vmem, vmem, anywhere, anywhere, anywhere],
        out_specs=(vmem, vmem),
        scratch_shapes=[
            pltpu.VMEM((2, 2, ROWS, ROWS), BF16),
            pltpu.VMEM((SUPER - 1, width, width), BF16),
            pltpu.VMEM((SUPER - 1, width, width), BF16),
            pltpu.VMEM((SUPER, width, 128), BF16),
            pltpu.VMEM((32, 128), F32),
            pltpu.VMEM((32, 128), F32),
            pltpu.VMEM((2, ny, PIECE, ROWS), BF16),
            pltpu.VMEM((nz * NX, PIECE, ROWS), BF16),
            pltpu.VMEM((nz, ROWS, PIECE), F32),
            pltpu.VMEM((nz, ROWS, PIECE), BF16),
            pltpu.VMEM((nz, ROWS, PIECE), BF16),
            pltpu.VMEM((ny, chain_rows, 128 * ny), BF16),
            pltpu.VMEM((ny - 1, chain_rows, 128 * ny), BF16),
            pltpu.VMEM((2, chain_rows, 128 * ny), F32),
            pltpu.VMEM((ny, chain_rows, 256), BF16),
            pltpu.VMEM((ROWS, 256), BF16),
            pltpu.VMEM((ROWS, 256), BF16),
            pltpu.VMEM((NX * nz, 32, 128), BF16),
            pltpu.VMEM((NX * nz - 1, 32, 128), BF16),
            pltpu.VMEM((32, 128), F32),
            pltpu.VMEM((ny, 32, 128), F32),
            pltpu.VMEM((nz, 32, 128), F32),
            pltpu.VMEM((NX * nz, 64, 128), BF16),
            pltpu.SemaphoreType.DMA((34,)),
            pltpu.SemaphoreType.DMA((2, nz)),
            pltpu.SemaphoreType.DMA((2, nz)),
            pltpu.SemaphoreType.DMA((nz,)),
            pltpu.SemaphoreType.DMA((ny,)),
            pltpu.SemaphoreType.DMA((nz,)),
        ],
        compiler_params=pltpu.CompilerParams(
            collective_id=0, has_side_effects=True, vmem_limit_bytes=53 * 1024 * 1024
        ),
        name="chain",
    )(
        panels.swapaxes(1, 2), listed.reshape(1, -1), trail_inverse, couplings,
        diag_terms.swapaxes(1, 2),
    )
    return panel.swapaxes(1, 2), diag.swapaxes(1, 2)


def solution(mesh):
    in_specs = (P("row", "col"), P(None, "row", "col"), P(), P(None, None, "col"), P())
    out_specs = (P(None, "row", "col"), P(None, None, "col"))
    return jax.shard_map(
        on_device, mesh=mesh, in_specs=in_specs, out_specs=out_specs, check_vma=False
    )
```

time: 109 us -> 103 us (0.945)
  Pallas kernels: 104 us -> 97 us
    pallas_call x1, Pallas kernels: 104 us -> 97 us  [on_device(): pl.pallas_call(functools.partial(kernel, ny), out_shape=(jax.ShapeDtypeSt...]
    unnamed x2 -> x8, local copies, waits for them, and re-layouts: 3.21 us -> 3.84 us
where the time goes in v3:
time: 103 us; the launch traced here: 102 us
  Pallas kernels  97 us (94%)
  local copies, waits for them, and re-layouts  3.84 us (4%)
    pallas_call x1, Pallas kernels, on_device(): pl.pallas_call(functools.partial(kernel, ny), out_shape=(jax.ShapeDtypeSt...  97 us
    unnamed x8, local copies, waits for them, and re-layouts  3.84 us

profile of v3, /device:TPU:1, one launch (start us, length us, event | category | flops | bytes accessed | tf_op | source)
XLA Modules:
  0.0 101.5 jit_solution(5394988234362384288)
XLA Ops:
  0.6 0.0 copy-start
  0.6 0.9 copy-done
  1.6 0.0 copy-start.1
  1.6 0.9 copy-done.1
  2.5 0.0 copy-start.2
  2.5 0.7 copy-done.2
  3.1 97.0 %chain.1 = (bf16[4,32,384]{2,1,0:T(8,128)(2,1)S(1)}, f32[4,32,512]{2,1,0:T(8,128)S(1)}) custom-call(bf16[4,32,384]{2,1,0:T(8,128)(2,1)S(1)} %bitcast.7, s32[1,64]{1,0:T(1,128)S(1)} %bitcast.9, bf16[384,768]{1,0:T(8,128)(2,1)} %trail_ref.1, bf16[3,512,512]{2,1,0:T(8,128)(2,1)} %coup_ref.1, f32[4,32,512]{2,1,0:T(8,128)S(1)} %bitcast.6), custom_call_target="tpu_custom_call" | custom-call | tf_op jit(solution)/shard_map/chain/pallas_call | solution.py:476
  100.2 0.6 copy.9
  100.8 0.7 copy.10
Async XLA Ops:
  0.6 1.0 copy-start
  1.6 0.9 copy-start.1
  2.5 0.7 copy-start.2

commit v4 on v3

--- a/solution.py
+++ b/solution.py
@@ -11,6 +11,7 @@
 NX = 4
 ROWS = 384
 PIECE = 128
+PARTS = 4
 LAG = 3
 ADD = 5
 MESH = pl.DeviceIdType.MESH
@@ -42,7 +43,7 @@
     ny,
     panels_ref, listed_ref, trail_ref, coup_ref, diag_ref,
     outp_ref, outd_ref,
-    tp, cc, ct, vst, dgo, dgs, mw, ms, part, out, got, sp, rb, ss, zs, zb, zo, ps, pb, ev, eb1, eb2, fb,
+    tp, cc, ct, vst, dgo, dgs, mw, ms, held, out, got, sp, rb, ss, zs, zb, zo, ps, pb, ev, eb1, eb2, fb,
     sem, zrecv, xrecv, precv, yrecv, frecv,
 ):
     nz = ny
@@ -66,9 +67,9 @@
     def wait_bytes(ref, semaphore):
         pltpu.make_async_copy(ref, ref, semaphore).wait()
 
-    (s_t, r_t, s_z, s_x, s_mw, s_p2, r_t2, s_eb, s_td, r_td, s_tp, r_tp, s_rs, r_rs, s_ss, r_ss, s_zb, r_zb,
+    (s_t, s_z, s_x, s_mw, s_p2, s_eb, s_td, r_td, s_tp, r_tp, s_rs, r_rs, s_ss, r_ss, s_zb, r_zb,
      s_mf, r_mf, s_zo, r_zo, s_p, r_p, s_e, r_e1, r_e2, s_f, r_f, s_dg, r_dg,
-     l_tp, l_cc, l_dg) = [sem.at[i] for i in range(34)]
+     l_tp, l_cc, l_dg) = [sem.at[i] for i in range(32)]
 
     barrier = pltpu.get_barrier_semaphore()
 
@@ -122,19 +123,19 @@
     )
 
     mine = mw.at[h, y]
-    landed = (r_t, r_t2)
-    halves = [pl.ds(64 * half, 64) for half in range(2)]
-
-    for half in range(2):
-        target = ms.at[y * NX + x, halves[half]]
+    size = PIECE // PARTS
+    parts = [pl.ds(size * part, size) for part in range(PARTS)]
+
+    for part in range(PARTS):
+        target = ms.at[y * NX + x, parts[part]]
 
         @pl.when(y != z)
         def _():
-            remote(mine.at[halves[half]], target, s_t, landed[half], dev(x, z, y, h)).start()
+            remote(mine.at[parts[part]], target, s_t, zrecv.at[part, 0], dev(x, z, y, h)).start()
 
         @pl.when(y == z)
         def _():
-            pltpu.make_async_copy(mine.at[halves[half]], target, landed[half]).start()
+            pltpu.make_async_copy(mine.at[parts[part]], target, zrecv.at[part, 0]).start()
 
     given = trail_ref.at[:, pl.ds(pl.multiple_of(given_side * ROWS, ROWS), ROWS)]
     remote(given, tp.at[h, 1], s_tp, r_tp, dev(pair, y, z, h)).start()
@@ -146,6 +147,102 @@
         return jnp.where(lax.rem(step, 2) == 1, half, mod(-half, nz))
 
     home = ms.at[z * NX + x]
+
+    def relay_piece(step, part):
+        slot = ms.at[mod(z - near(step), nz) * NX + x, parts[part]]
+        z_next = mod(z + jnp.where(lax.rem(step, 2) == 1, 1, -1), nz)
+        wait_bytes(slot, zrecv.at[part, step])
+
+        @pl.when(step == 0)
+        def _():
+            remote(slot, slot, s_z, zrecv.at[part, 1], dev(x, y, mod(z + 1, nz), h)).start()
+
+        @pl.when(step < nz - 2)
+        def _():
+            remote(slot, slot, s_z, zrecv.at[part, step + 2], dev(x, y, z_next, h)).start()
+
+        remote(slot, slot, s_x, xrecv.at[part, step], dev(3 - x, y, z, h)).start()
+
+    def relay_wide(step):
+        wide = mw.at[h, mod(y - near(step), ny)]
+        y_next = mod(y + jnp.where(lax.rem(step, 2) == 1, 1, -1), ny)
+
+        @pl.when(step > 0)
+        def _():
+            wait_bytes(wide, yrecv.at[step])
+
+        @pl.when(step == 0)
+        def _():
+            remote(wide, wide, s_mw, yrecv.at[1], dev(x, mod(y + 1, ny), z, h)).start()
+
+        @pl.when(step < ny - 2)
+        def _():
+            remote(wide, wide, s_mw, yrecv.at[step + 2], dev(x, y_next, z, h)).start()
+
+    @pl.loop(0, nz + ADD)
+    def _(step):
+        @pl.when(step < nz)
+        def _():
+            for part in range(PARTS // 2):
+                relay_piece(step, part)
+
+        @pl.when(jnp.logical_and(step >= 1, step <= nz))
+        def _():
+            for part in range(PARTS // 2, PARTS):
+                relay_piece(step - 1, part)
+
+        @pl.when(step < nz)
+        def _():
+            relay_wide(step)
+
+        @pl.when(step == LAG - 2)
+        def _():
+            own_tp.wait()
+            wait_bytes(tp.at[0, 0], r_tp)
+            remote(tp.at[h], tp.at[h], s_td, r_td, dev(x, y, z, sibling)).start()
+
+        @pl.when(step == LAG)
+        def _():
+            wait_bytes(tp.at[0], r_td)
+
+        @pl.when(jnp.logical_and(step >= LAG, step < nz + LAG))
+        def _():
+            at = step - LAG
+            chunk = mod(z - near(at), nz)
+            for part in range(PARTS):
+                wait_bytes(home.at[parts[part]], xrecv.at[part, at])
+            sums = [None, None]
+            for core in range(2):
+                piece = ms[chunk * NX + 2 * core + side_of(core)]
+                for rows in range(2):
+                    term = lax.dot_general(
+                        tp[core, rows], piece, NT_DIMS, preferred_element_type=F32
+                    )
+                    sums[rows] = term if core == 0 else sums[rows] + term
+            held[chunk] = sums[0]
+            out[chunk] = sums[1].astype(BF16)
+            remote(out.at[chunk], got.at[chunk], s_p2, precv.at[at], dev(pair, y, z, h)).start()
+
+        @pl.when(step >= ADD)
+        def _():
+            at = step - ADD
+            chunk = mod(z - near(at), nz)
+            wait_bytes(got.at[chunk], precv.at[at])
+            total = held[chunk] + got[chunk].astype(F32)
+            total = total.astype(BF16)
+            lanes = pl.ds(pl.multiple_of(chunk * PIECE, PIECE), PIECE)
+            for yy in range(ny):
+                sp[yy, :, lanes] = total[chain_rows * yy:chain_rows * (yy + 1)]
+
+            for i in range(1, ny):
+                to = mod(y + i, ny)
+                remote(
+                    sp.at[to, :, lanes], rb.at[i - 1, :, lanes], s_rs, r_rs, dev(x, to, z, h)
+                ).start()
+
+    send_mf = remote(mw.at[h], mw.at[h], s_mf, r_mf, dev(x, y, z, sibling))
+    send_mf.start()
+
     own_cc.wait()
     wide_eye = jnp.where(iota((width, width), 0) == iota((width, width), 1), 1.0, 0.0)
     wide_eye = wide_eye.astype(BF16)
@@ -168,98 +265,6 @@
     both = jnp.concatenate([dgo[...], dgs[...], jnp.zeros((64, 128), F32)], axis=0)
     both = jnp.where(lax.rem(z, 2) == 0, both, swap_halves(both)).T
     diag_packed = jnp.where(iota((32, 128), 1) < 64, both[0:32], swap_halves(both[32:64]))
-
-    own_tp.wait()
-    wait_bytes(tp.at[0, 0], r_tp)
-    remote(tp.at[h], tp.at[h], s_td, r_td, dev(x, y, z, sibling)).start()
-    wait_bytes(tp.at[0], r_td)
-
-    def relay_piece(step, half):
-        slot = ms.at[mod(z - near(step), nz) * NX + x, halves[half]]
-        z_next = mod(z + jnp.where(lax.rem(step, 2) == 1, 1, -1), nz)
-
-        @pl.when(step > 0)
-        def _():
-            wait_bytes(slot, zrecv.at[half, step])
-
-        @pl.when(step == 0)
-        def _():
-            wait_bytes(slot, landed[half])
-            remote(slot, slot, s_z, zrecv.at[half, 1], dev(x, y, mod(z + 1, nz), h)).start()
-
-        @pl.when(step < nz - 2)
-        def _():
-            remote(slot, slot, s_z, zrecv.at[half, step + 2], dev(x, y, z_next, h)).start()
-
-        remote(slot, slot, s_x, xrecv.at[half, step], dev(3 - x, y, z, h)).start()
-
-    def relay_wide(step):
-        wide = mw.at[h, mod(y - near(step), ny)]
-        y_next = mod(y + jnp.where(lax.rem(step, 2) == 1, 1, -1), ny)
-
-        @pl.when(step > 0)
-        def _():
-            wait_bytes(wide, yrecv.at[step])
-
-        @pl.when(step == 0)
-        def _():
-            remote(wide, wide, s_mw, yrecv.at[1], dev(x, mod(y + 1, ny), z, h)).start()
-
-        @pl.when(step < ny - 2)
-        def _():
-            remote(wide, wide, s_mw, yrecv.at[step + 2], dev(x, y_next, z, h)).start()
-
-    @pl.loop(0, nz + ADD)
-    def _(step):
-        @pl.when(step < nz)
-        def _():
-            relay_piece(step, 0)
-
-        @pl.when(jnp.logical_and(step >= 1, step <= nz))
-        def _():
-            relay_piece(step - 1, 1)
-
-        @pl.when(step < nz)
-        def _():
-            relay_wide(step)
-
-        @pl.when(jnp.logical_and(step >= LAG, step < nz + LAG))
-        def _():
-            at = step - LAG
-            chunk = mod(z - near(at), nz)
-            for half in range(2):
-                wait_bytes(home.at[halves[half]], xrecv.at[half, at])
-            sums = [None, None]
-            for core in range(2):
-                piece = ms[chunk * NX + 2 * core + side_of(core)]
-                for rows in range(2):
-                    term = lax.dot_general(
-                        tp[core, rows], piece, NT_DIMS, preferred_element_type=F32
-                    )
-                    sums[rows] = term if core == 0 else sums[rows] + term
-            part[chunk] = sums[0]
-            out[chunk] = sums[1].astype(BF16)
-            remote(out.at[chunk], got.at[chunk], s_p2, precv.at[at], dev(pair, y, z, h)).start()
-
-        @pl.when(step >= ADD)
-        def _():
-            at = step - ADD
-            chunk = mod(z - near(at), nz)
-            wait_bytes(got.at[chunk], precv.at[at])
-            total = part[chunk] + got[chunk].astype(F32)
-            total = total.astype(BF16)
-            lanes = pl.ds(pl.multiple_of(chunk * PIECE, PIECE), PIECE)
-            for yy in range(ny):
-                sp[yy, :, lanes] = total[chain_rows * yy:chain_rows * (yy + 1)]
-
-            for i in range(1, ny):
-                to = mod(y + i, ny)
-                remote(
-                    sp.at[to, :, lanes], rb.at[i - 1, :, lanes], s_rs, r_rs, dev(x, to, z, h)
-                ).start()
-
-    send_mf = remote(mw.at[h], mw.at[h], s_mf, r_mf, dev(x, y, z, sibling))
-    send_mf.start()
 
     wait_bytes(rb, r_rs)
     for t in range(ny):
@@ -339,7 +344,11 @@
                 packed = jnp.where(low32, swap_halves(upper), lower)
             ps[k * nz + zz] = packed.astype(BF16)
 
-    for i in range(1, NX * nz):
+    far_first = sorted(
+        range(1, NX * nz),
+        key=lambda i: (-min(i % nz, nz - i % nz), -min(i // nz, NX - i // nz), i),
+    )
+    for i in far_first:
         xx, zz = mod(x + i // nz, NX), mod(z + i % nz, nz)
         remote(ps.at[xx * nz + zz], pb.at[i - 1], s_p, r_p, dev(xx, y, zz, h)).start()
 
@@ -505,9 +514,9 @@
             pltpu.VMEM((ny, 32, 128), F32),
             pltpu.VMEM((nz, 32, 128), F32),
             pltpu.VMEM((NX * nz, 64, 128), BF16),
-            pltpu.SemaphoreType.DMA((34,)),
-            pltpu.SemaphoreType.DMA((2, nz)),
-            pltpu.SemaphoreType.DMA((2, nz)),
+            pltpu.SemaphoreType.DMA((32,)),
+            pltpu.SemaphoreType.DMA((PARTS, nz)),
+            pltpu.SemaphoreType.DMA((PARTS, nz)),
             pltpu.SemaphoreType.DMA((nz,)),
             pltpu.SemaphoreType.DMA((ny,)),
             pltpu.SemaphoreType.DMA((nz,)),

time: 103 us -> 101 us (0.981); the launches traced: 102 us -> 101 us
  no operation moved by 1% of the time
where the time goes in v4:
time: 101 us
  Pallas kernels  96.2 us (95%)
  local copies, waits for them, and re-layouts  3.84 us (4%)
    pallas_call x1, Pallas kernels, on_device(): pl.pallas_call(functools.partial(kernel, ny), out_shape=(jax.ShapeDtypeSt...  96.2 us
    unnamed x8, local copies, waits for them, and re-layouts  3.84 us

profile of v4, /device:TPU:1, one launch (start us, length us, event | category | flops | bytes accessed | tf_op | source)
XLA Modules:
  0.0 100.7 jit_solution(9699712020978507367)
XLA Ops:
  0.6 0.0 copy-start
  0.6 0.9 copy-done
  1.6 0.0 copy-start.1
  1.6 0.9 copy-done.1
  2.5 0.0 copy-start.2
  2.5 0.7 copy-done.2
  3.1 96.2 %chain.1 = (bf16[4,32,384]{2,1,0:T(8,128)(2,1)S(1)}, f32[4,32,512]{2,1,0:T(8,128)S(1)}) custom-call(bf16[4,32,384]{2,1,0:T(8,128)(2,1)S(1)} %bitcast.7, s32[1,64]{1,0:T(1,128)S(1)} %bitcast.9, bf16[384,768]{1,0:T(8,128)(2,1)} %trail_ref.1, bf16[3,512,512]{2,1,0:T(8,128)(2,1)} %coup_ref.1, f32[4,32,512]{2,1,0:T(8,128)S(1)} %bitcast.6), custom_call_target="tpu_custom_call" | custom-call | tf_op jit(solution)/shard_map/chain/pallas_call | solution.py:485
  99.4 0.6 copy.9
  100.0 0.7 copy.10
Async XLA Ops:
  0.6 1.0 copy-start
  1.6 0.9 copy-start.1
  2.5 0.7 copy-start.2

commit v5 on v4

--- a/solution.py
+++ b/solution.py
@@ -12,8 +12,8 @@
 ROWS = 384
 PIECE = 128
 PARTS = 4
-LAG = 3
-ADD = 5
+LAG = 2
+ADD = 4
 MESH = pl.DeviceIdType.MESH
 F32 = jnp.float32
 BF16 = jnp.bfloat16
@@ -183,13 +183,8 @@
     def _(step):
         @pl.when(step < nz)
         def _():
-            for part in range(PARTS // 2):
+            for part in range(PARTS):
                 relay_piece(step, part)
-
-        @pl.when(jnp.logical_and(step >= 1, step <= nz))
-        def _():
-            for part in range(PARTS // 2, PARTS):
-                relay_piece(step - 1, part)
 
         @pl.when(step < nz)
         def _():
@@ -522,7 +517,7 @@
             pltpu.SemaphoreType.DMA((nz,)),
         ],
         compiler_params=pltpu.CompilerParams(
-            collective_id=0, has_side_effects=True, vmem_limit_bytes=53 * 1024 * 1024
+            collective_id=0, has_side_effects=True, vmem_limit_bytes=53 * 1024 * 1024 + 256 * 1024
         ),
         name="chain",
     )(

time: 101 us -> 99.1 us (0.981)
  Pallas kernels: 96.2 us -> 95.1 us
    pallas_call x1, Pallas kernels: 96.2 us -> 95.1 us  [on_device(): pl.pallas_call(functools.partial(kernel, ny), out_shape=(jax.ShapeDtypeSt...]
    unnamed x8 -> x6, local copies, waits for them, and re-layouts: 3.84 us -> 2.89 us
where the time goes in v5:
time: 99.1 us; the launch traced here: 98.7 us
  Pallas kernels  95.1 us (96%)
  local copies, waits for them, and re-layouts  2.89 us (3%)
    pallas_call x1, Pallas kernels, on_device(): pl.pallas_call(functools.partial(kernel, ny), out_shape=(jax.ShapeDtypeSt...  95.1 us
    unnamed x6, local copies, waits for them, and re-layouts  2.89 us

profile of v5, /device:TPU:1, one launch (start us, length us, event | category | flops | bytes accessed | tf_op | source)
XLA Modules:
  0.0 98.7 jit_solution(14433798934852366469)
XLA Ops:
  0.6 0.0 copy-start
  0.6 0.9 copy-done
  1.5 0.0 copy-start.1
  1.5 0.7 copy-done.1
  2.2 95.1 %chain.1 = (bf16[4,32,384]{2,1,0:T(8,128)(2,1)S(1)}, f32[4,32,512]{2,1,0:T(8,128)S(1)}) custom-call(bf16[4,32,384]{2,1,0:T(8,128)(2,1)S(1)} %bitcast.6, s32[1,64]{1,0:T(1,128)S(1)} %bitcast.8, bf16[384,768]{1,0:T(8,128)(2,1)} %trail_ref.1, bf16[3,512,512]{2,1,0:T(8,128)(2,1)} %coup_ref.1, f32[4,32,512]{2,1,0:T(8,128)} %bitcast.9), custom_call_target="tpu_custom_call" | custom-call | tf_op jit(solution)/shard_map/chain/pallas_call | solution.py:480
  97.3 0.6 copy.9
  98.0 0.7 copy.10
Async XLA Ops:
  0.6 0.9 copy-start
  1.5 0.7 copy-start.1

commit v6 on v5

--- a/solution.py
+++ b/solution.py
@@ -79,7 +79,7 @@
     greet(dev(x, y, z, sibling))
     for step in (1, nz - 1) if nz > 2 else (1,):
         greet(dev(x, y, mod(z + step, nz), h))
-    for step in range(1, NX):
+    for step in (1, NX - 1):
         greet(dev(mod(x + step, NX), y, z, h))
     for step in range(1, ny):
         greet(dev(x, mod(y + step, ny), z, h))
@@ -119,7 +119,7 @@
         mw[h, y, 32 * k:32 * (k + 1), :] = (turned * piece_mask).astype(BF16)
 
     pl.semaphore_wait(
-        barrier, min(2, nz - 1) + NX + ny - 1 + jnp.where(y != z, 1, 0)
+        barrier, min(2, nz - 1) + NX - 1 + ny - 1 + jnp.where(y != z, 1, 0)
     )
 
     mine = mw.at[h, y]

time: 99.1 us -> 99.3 us (level); the launches traced: 98.7 us -> 97.8 us
  no operation moved by 1% of the time
where the time goes in v6:
time: 99.3 us; the launch traced here: 97.8 us
  Pallas kernels  94.3 us (95%)
  local copies, waits for them, and re-layouts  2.89 us (3%)
    pallas_call x1, Pallas kernels, on_device(): pl.pallas_call(functools.partial(kernel, ny), out_shape=(jax.ShapeDtypeSt...  94.3 us
    unnamed x6, local copies, waits for them, and re-layouts  2.89 us

profile of v6, /device:TPU:1, one launch (start us, length us, event | category | flops | bytes accessed | tf_op | source)
XLA Modules:
  0.0 97.8 jit_solution(12985860528875803294)
XLA Ops:
  0.6 0.0 copy-start
  0.6 0.9 copy-done
  1.5 0.0 copy-start.1
  1.5 0.7 copy-done.1
  2.2 94.3 %chain.1 = (bf16[4,32,384]{2,1,0:T(8,128)(2,1)S(1)}, f32[4,32,512]{2,1,0:T(8,128)S(1)}) custom-call(bf16[4,32,384]{2,1,0:T(8,128)(2,1)S(1)} %bitcast.6, s32[1,64]{1,0:T(1,128)S(1)} %bitcast.8, bf16[384,768]{1,0:T(8,128)(2,1)} %trail_ref.1, bf16[3,512,512]{2,1,0:T(8,128)(2,1)} %coup_ref.1, f32[4,32,512]{2,1,0:T(8,128)} %bitcast.9), custom_call_target="tpu_custom_call" | custom-call | tf_op jit(solution)/shard_map/chain/pallas_call | solution.py:480
  96.5 0.6 copy.9
  97.1 0.7 copy.10
Async XLA Ops:
  0.6 0.9 copy-start
  1.5 0.7 copy-start.1
